TPU v7x, 128 devices: a whole 4x4x4 slice. The times are simulated.
128 devices in a mesh: seq: 16 (over x_hi, y, core), blk: 8 (over x_lo, z).
Axes of the slice: x: 4 (x_hi: 2, x_lo: 2; x = x_hi * 2 + x_lo), y: 4, z: 4, core: 2. Of those that a mesh axis runs over, the one named last changes fastest.
Arguments:
- tokens: bfloat16 [16384, 1536], P(('seq', 'blk')), may hold values from -6 to 6
- boundary: int32 [16384], P(('seq', 'blk')), may hold values from 0 to 1, as said below
- heads_in: bfloat16 [1536, 3, 1536], P(None, None, 'blk')
- heads_out: bfloat16 [1536, 1536], P('blk'), may hold values from -0.15625 to 0.15625
- gate_up: bfloat16 [1536, 2, 4096], P(None, None, 'blk'), may hold values from -0.15625 to 0.15625
- down_weight: bfloat16 [4096, 1536], P('blk'), may hold values from -0.09375 to 0.09375
- widen: bfloat16 [1536, 4096], P(None, 'blk'), may hold values from -0.15625 to 0.15625
- heads_in_two: bfloat16 [4096, 3, 4096], P(None, None, 'blk')
- heads_out_two: bfloat16 [4096, 4096], P('blk'), may hold values from -0.09375 to 0.09375
Outputs:
- level_one: bfloat16 [16384, 1536], P(('seq', 'blk'))
- level_two: bfloat16 [8192, 4096], P('seq', 'blk')
Inputs may be any that keep to these rules, and one draw needn't show every extreme that they name: `boundary`: each aligned block of 1024 consecutive rows holds between 256 and 512 ones, and some block holds exactly 512.
All inputs are finite; a program needn't handle non-finite values.
Results may differ from a plain program's by a relative error of at most 0.04.
Values may be sent and summed in bfloat16 or wider, within the bound.
No kernel may reach another device: no remote copies, remote signals or barrier semaphores. Data moves between devices by JAX's collectives and lax.ppermute only.
A program may use at most 128 MiB of HBM per device.

v0:
```python
import jax
import jax.numpy as jnp
from jax import lax
from jax.sharding import PartitionSpec as P

D1 = 1536
H1 = 24
D2 = 4096
H2 = 32
WIN = 512


def from_behind(value, axis, steps):
    count = lax.axis_size(axis)
    first, last = (max(0, -steps), min(count, count - steps))
    return lax.ppermute(value, axis, [(source, source + steps) for source in range(first, last)])


def normalize(values):
    floats = values.astype(jnp.float32)
    return floats * lax.rsqrt(jnp.mean(floats * floats, axis=-1, keepdims=True) + 1e-06)


def place_rows(slot_ids, marks, row_block, capacity):
    targets = jnp.arange(capacity, dtype=jnp.int32)
    selector = ((slot_ids[None, :] == targets[:, None]) & (marks[None, :] == 1)).astype(
        jnp.bfloat16
    )
    return jnp.dot(selector, row_block, preferred_element_type=jnp.float32)


def window_attend(normed_rows, heads_in, seq_position):
    group_rows = normed_rows.shape[0]
    queries = jnp.dot(normed_rows, heads_in[:, 0, :], preferred_element_type=jnp.float32).astype(
        jnp.bfloat16
    )
    keys_all = jnp.dot(normed_rows, heads_in[:, 1, :], preferred_element_type=jnp.float32).astype(
        jnp.bfloat16
    )
    values_all = jnp.dot(normed_rows, heads_in[:, 2, :], preferred_element_type=jnp.float32).astype(
        jnp.bfloat16
    )
    local_width = queries.shape[1]
    head_size = D1 // H1
    head_count = local_width // head_size
    edge = jnp.stack([keys_all[group_rows - WIN :], values_all[group_rows - WIN :]])
    earlier = from_behind(edge, "seq", 1)
    keys_ext = jnp.concatenate([earlier[0], keys_all], axis=0)
    values_ext = jnp.concatenate([earlier[1], values_all], axis=0)
    block = min(512, group_rows)
    row_base = seq_position * group_rows

    def one_block(block_index):
        first = block_index * block
        query_block = lax.dynamic_slice_in_dim(queries, first, block).reshape(
            block, head_count, head_size
        )
        key_block = lax.dynamic_slice_in_dim(keys_ext, first, block + WIN).reshape(
            block + WIN, head_count, head_size
        )
        value_block = lax.dynamic_slice_in_dim(values_ext, first, block + WIN).reshape(
            block + WIN, head_count, head_size
        )
        scores = jnp.einsum(
            "qhd,khd->hqk", query_block, key_block, preferred_element_type=jnp.float32
        ) * head_size ** (-0.5)
        query_pos = first + jnp.arange(block, dtype=jnp.int32)
        key_pos = first - WIN + jnp.arange(block + WIN, dtype=jnp.int32)
        allowed = (
            (key_pos[None, :] <= query_pos[:, None])
            & (key_pos[None, :] > query_pos[:, None] - WIN)
            & (row_base + key_pos[None, :] >= 0)
        )
        scores = jnp.where(allowed[None], scores, -1e30)
        largest = jnp.max(scores, axis=-1, keepdims=True)
        weights = jnp.where(allowed[None], jnp.exp(scores - largest), 0.0)
        totals = jnp.sum(weights, axis=-1)
        mixed = (
            jnp.einsum(
                "hqk,khd->qhd",
                weights.astype(jnp.bfloat16),
                value_block,
                preferred_element_type=jnp.float32,
            )
            / totals.T[:, :, None]
        )
        return mixed.astype(jnp.bfloat16).reshape(block, local_width)

    blocks = lax.map(one_block, jnp.arange(group_rows // block, dtype=jnp.int32))
    return blocks.reshape(group_rows, local_width)


def causal_folder(queries, seq_position, head_size):
    capacity, local_width = queries.shape
    head_count = local_width // head_size
    query_heads = queries.reshape(capacity, head_count, head_size)
    query_pos = seq_position * capacity + jnp.arange(capacity, dtype=jnp.int32)

    def absorb(totals, key_block, value_block, valid_block, offset):
        running_max, running_sum, accumulated = totals
        key_count = key_block.shape[0]
        scores = jnp.einsum(
            "qhd,khd->hqk",
            query_heads,
            key_block.reshape(key_count, head_count, head_size),
            preferred_element_type=jnp.float32,
        ) * head_size ** (-0.5)
        key_pos = offset + jnp.arange(key_count, dtype=jnp.int32)
        allowed = (key_pos[None, :] <= query_pos[:, None]) & (valid_block[None, :] > 0.5)
        scores = jnp.where(allowed[None], scores, -1e30)
        new_max = jnp.maximum(running_max, jnp.max(scores, axis=-1))
        decay = jnp.exp(running_max - new_max)
        weights = jnp.where(allowed[None], jnp.exp(scores - new_max[:, :, None]), 0.0)
        running_sum = running_sum * decay + jnp.sum(weights, axis=-1)
        value_floats = value_block.reshape(key_count, head_count, head_size).astype(jnp.float32)
        update = jnp.einsum(
            "hqk,khd->qhd",
            weights,
            value_floats,
            precision=lax.Precision.HIGHEST,
            preferred_element_type=jnp.float32,
        )
        accumulated = accumulated * decay.T[:, :, None] + update
        return (new_max, running_sum, accumulated)

    def fold_piece(totals, shard_piece, offset):
        key_piece, value_piece, valid_piece = shard_piece
        piece_rows = key_piece.shape[0]
        step_rows = 512

        def inner(step_index, inner_totals):
            first = step_index * step_rows
            return absorb(
                inner_totals,
                lax.dynamic_slice_in_dim(key_piece, first, step_rows),
                lax.dynamic_slice_in_dim(value_piece, first, step_rows),
                lax.dynamic_slice_in_dim(valid_piece, first, step_rows),
                first,
            )

        return lax.fori_loop(0, piece_rows // step_rows, inner, totals)

    initial = (
        jnp.full((head_count, capacity), -1e30, jnp.float32),
        jnp.zeros((head_count, capacity), jnp.float32),
        jnp.zeros((capacity, head_count, head_size), jnp.float32),
    )
    return (fold_piece, initial)


def per_device(
    tokens, boundary, heads_in, heads_out, gate_up, down_weight, widen, heads_in_two, heads_out_two
):
    block_count = lax.axis_size("blk")
    seq_position = lax.axis_index("seq")
    row_count = tokens.shape[0]
    group_rows = row_count * block_count
    capacity = group_rows // 2
    group_marks = lax.all_gather(boundary, "blk", axis=0, tiled=True)
    slot_ids = jnp.cumsum(group_marks) - 1
    span_count = jnp.sum(group_marks)
    normed = normalize(tokens).astype(jnp.bfloat16)
    whole_normed = lax.all_gather(normed, "blk", axis=0, tiled=True)
    attended = window_attend(whole_normed, heads_in, seq_position)
    attn_partial = jnp.dot(attended, heads_out, preferred_element_type=jnp.float32)
    attn_reduced = lax.psum_scatter(
        attn_partial.astype(jnp.bfloat16), "blk", scatter_dimension=0, tiled=True
    ).astype(jnp.float32)
    mid_stream = (tokens.astype(jnp.float32) + attn_reduced).astype(jnp.bfloat16)
    normed_mid = normalize(mid_stream).astype(jnp.bfloat16)
    whole_mid = lax.all_gather(normed_mid, "blk", axis=0, tiled=True)
    gate_proj = jnp.dot(whole_mid, gate_up[:, 0, :], preferred_element_type=jnp.float32)
    up_proj = jnp.dot(whole_mid, gate_up[:, 1, :], preferred_element_type=jnp.float32)
    hidden = (jax.nn.silu(gate_proj) * up_proj).astype(jnp.bfloat16)
    mlp_partial = jnp.dot(hidden, down_weight, preferred_element_type=jnp.float32)
    mlp_reduced = lax.psum_scatter(
        mlp_partial.astype(jnp.bfloat16), "blk", scatter_dimension=0, tiled=True
    ).astype(jnp.float32)
    level_one = (mid_stream.astype(jnp.float32) + mlp_reduced).astype(jnp.bfloat16)
    placed = place_rows(
        slot_ids, group_marks, lax.all_gather(level_one, "blk", axis=0, tiled=True), capacity
    )
    pooled = placed.astype(jnp.bfloat16)
    wide_cols = jnp.dot(pooled, widen, preferred_element_type=jnp.float32).astype(jnp.bfloat16)
    wide = lax.all_gather(wide_cols, "blk", axis=1, tiled=True)
    normed_two = normalize(wide).astype(jnp.bfloat16)
    queries_two = jnp.dot(
        normed_two, heads_in_two[:, 0, :], preferred_element_type=jnp.float32
    ).astype(jnp.bfloat16)
    keys_two = jnp.dot(
        normed_two, heads_in_two[:, 1, :], preferred_element_type=jnp.float32
    ).astype(jnp.bfloat16)
    values_two = jnp.dot(
        normed_two, heads_in_two[:, 2, :], preferred_element_type=jnp.float32
    ).astype(jnp.bfloat16)
    validity = (jnp.arange(capacity, dtype=jnp.int32) < span_count).astype(jnp.float32)
    head_size = D2 // H2
    fold_piece, initial = causal_folder(queries_two, seq_position, head_size)
    running_max, running_sum, accumulated = fold_piece(
        initial,
        (
            lax.all_gather(keys_two, "seq", axis=0, tiled=True),
            lax.all_gather(values_two, "seq", axis=0, tiled=True),
            lax.all_gather(validity.astype(jnp.bfloat16), "seq", axis=0, tiled=True),
        ),
        jnp.int32(0),
    )
    attended_two = (
        (accumulated / running_sum.T[:, :, None])
        .astype(jnp.bfloat16)
        .reshape(capacity, queries_two.shape[1])
    )
    out_partial = jnp.dot(attended_two, heads_out_two, preferred_element_type=jnp.float32)
    out_reduced = lax.psum_scatter(
        out_partial.astype(jnp.bfloat16), "blk", scatter_dimension=1, tiled=True
    ).astype(jnp.float32)
    level_two = ((wide_cols.astype(jnp.float32) + out_reduced) * validity[:, None]).astype(
        jnp.bfloat16
    )
    return (level_one, level_two)


def solution(mesh):
    placed = (
        P(("seq", "blk"), None),
        P(("seq", "blk")),
        P(None, None, "blk"),
        P("blk", None),
        P(None, None, "blk"),
        P("blk", None),
        P(None, "blk"),
        P(None, None, "blk"),
        P("blk", None),
    )
    return jax.shard_map(
        per_device,
        mesh=mesh,
        in_specs=placed,
        out_specs=(P(("seq", "blk"), None), P("seq", "blk")),
        check_vma=False,
    )
```

profile of v0, /device:TPU:6, one launch (start us, length us, event | category | flops | bytes accessed | tf_op | source)
XLA Modules:
  0.0 781.2 jit_solution(14866991272836586146)
XLA Ops:
  10.5 46.1 %all-gather.9.cloned.1.call-done = bf16[1024,1536]{1,0:T(8,128)(2,1)} async-done(((bf16[128,1536]{1,0:T(8,128)(2,1)}), bf16[1024,1536]{1,0:T(8,128)(2,1)}) %all-gather.9.cloned.1.call-update) | async-done | bytes 3145744 | tf_op jit(solution)/shard_map/all_gather | solution.py:163
  68.2 6.8 collective-permute-done
  75.1 26.2 %while.31 = (s32[]{:T(128)}, bf16[2,512,192]{1,2,0:T(8,128)(2,1)}, s32[2]{0:T(128)S(1)}, bf16[1536,192]{0,1:T(8,128)(2,1)S(1)}, s32[]{:T(128)}, /*index=5*/bf16[...) while((s32[]{:T(128)}, bf16[2,512,192]{1,2,0:T(8,128)(2,1)}, ...), condition=%wide.region_4.5_spmd, body=%wide.region_1.0_spmd.sunk | while | flops 414390272 | bytes 10910452 | solution.py:89
  106.2 43.5 %reduce-scatter.4.cloned.1.call-done = bf16[128,1536]{1,0:T(8,128)(2,1)} async-done(((bf16[1024,1536]{1,0:T(8,128)(2,1)}), bf16[128,1536]{1,0:T(8,128)(2,1)}) %reduce-scatter.4.cloned.1.call-update) | async-done | bytes 393232 | tf_op jit(solution)/shard_map/reduce_scatter | solution.py:166
  153.1 9.5 %fusion.83 = (bf16[1536,1,512]{2,1,0:T(2,128)(2,1)}, bf16[1536,1,512]{2,1,0:T(2,128)(2,1)}) fusion(bf16[1536,2,512]{2,1,0:T(2,128)(2,1)} %param.17), kind=kLoop, calls=%fused_computation.122 | loop fusion | bytes 6291456 | tf_op jit(solution)/shard_map/slice | solution.py:173
  162.6 34.3 %all-gather.11.cloned.1.call-done = bf16[1024,1536]{1,0:T(8,128)(2,1)} async-done(((bf16[128,1536]{1,0:T(8,128)(2,1)}), bf16[1024,1536]{1,0:T(8,128)(2,1)}) %all-gather.11.cloned.1.call-update) | async-done | bytes 3145744 | tf_op jit(solution)/shard_map/all_gather | solution.py:171
  202.9 8.7 %convolution_convert_fusion.2 = bf16[1024,1536]{1,0:T(8,128)(2,1)} fusion(bf16[512,1536]{1,0:T(8,128)(2,1)S(1)} %copy-done, f32[1024,512]{1,0:T(8,128)} %fusion.50, bf16[1024,1536]{1,0:T(8,128)(2,1)} %all-gather.11.cloned.1.call-done, bf16[1536,1,512]{2,1,0:T(2,128)(2,1)} %get-tuple-element.375), kind=kOutput, calls=%fused_computation.67 | convolution fusion | flops 3225944064 | bytes 11534336 | tf_op jit(solution)/shard_map/dot_general | solution.py:175
  211.7 45.8 %reduce-scatter.6.cloned.1.call-done = bf16[128,1536]{1,0:T(8,128)(2,1)} async-done(((bf16[1024,1536]{1,0:T(8,128)(2,1)}), bf16[128,1536]{1,0:T(8,128)(2,1)}) %reduce-scatter.6.cloned.1.call-update) | async-done | bytes 393232 | tf_op jit(solution)/shard_map/reduce_scatter | solution.py:176
  259.4 17.5 %all-gather = s32[8,1,128]{2,1,0:T(1,128)S(1)} all-gather(s32[1,1,128]{2,1,0:T(1,128)S(1)} %bitcast.165), channel_id=1, replica_groups=mesh['seq'=16,'blk'=8] {'blk'}, dimensions={0}, use_global_device_ids=true | all-gather | bytes 4608 | tf_op jit(solution)/shard_map/all_gather | solution.py:159
  277.5 26.2 %all-gather.13.cloned.1.call-done = bf16[1024,1536]{1,0:T(8,128)(2,1)} async-done(((bf16[128,1536]{1,0:T(8,128)(2,1)}), bf16[1024,1536]{1,0:T(8,128)(2,1)}) %all-gather.13.cloned.1.call-update) | async-done | bytes 3145744 | tf_op jit(solution)/shard_map/all_gather | solution.py:181
  309.5 52.5 %all-gather.15.cloned.1.call-done = bf16[512,4096]{1,0:T(8,128)(2,1)} async-done(((bf16[512,512]{1,0:T(8,128)(2,1)}), bf16[512,4096]{1,0:T(8,128)(2,1)}) %all-gather.15.cloned.1.call-update) | async-done | bytes 4194320 | tf_op jit(solution)/shard_map/all_gather | solution.py:185
  370.9 6.6 fusion.51
  378.9 22.7 %all-gather.1 = bf16[16,1,512]{2,1,0:T(2,128)(2,1)S(1)} all-gather(bf16[1,1,512]{2,1,0:T(2,128)(2,1)S(1)} %reshape.263), channel_id=1, replica_groups=mesh['seq'=16,'blk'=8] {'seq'}, dimensions={0}, use_global_device_ids=true | all-gather | bytes 17408 | tf_op jit(solution)/shard_map/all_gather | solution.py:204
  407.8 33.9 %all-gather.19.cloned.1.call-done = bf16[8192,512]{1,0:T(8,128)(2,1)} async-done(((bf16[512,512]{1,0:T(8,128)(2,1)}), bf16[8192,512]{1,0:T(8,128)(2,1)}) %all-gather.19.cloned.1.call-update) | async-done | bytes 8388624 | tf_op jit(solution)/shard_map/all_gather | solution.py:203
  441.7 73.2 %all-gather.17.cloned.1.call-done = bf16[8192,512]{1,0:T(8,128)(2,1)} async-done(((bf16[512,512]{1,0:T(8,128)(2,1)}), bf16[8192,512]{1,0:T(8,128)(2,1)}) %all-gather.17.cloned.1.call-update) | async-done | bytes 8388624 | tf_op jit(solution)/shard_map/all_gather | solution.py:202
  514.9 197.6 %while.32 = (s32[]{:T(128)}, f32[4,512]{1,0:T(4,128)S(1)}, f32[4,512]{1,0:T(4,128)S(1)}, f32[512,4,128]{0,2,1:T(8,128)}, bf16[8192]{0:T(1024)(128)(2,1)S(1)}, /*...) while((s32[]{:T(128)}, f32[4,512]{1,0:T(4,128)S(1)}, ...), condition=%wide.region_15.16_spmd.clone, body=%wide.region_12.15_spmd.clone.sunk | while | flops 1892956672 | bytes 38414560 | solution.py:141
  531.9 6.3 fusion.132
  544.3 6.3 fusion.132
  556.7 6.3 fusion.132
  569.1 6.3 fusion.132
  581.4 6.3 fusion.132
  593.8 6.3 fusion.132
  618.5 6.3 fusion.132
  630.9 6.3 fusion.132
  643.3 6.3 fusion.132
  655.7 6.3 fusion.132
  668.0 6.3 fusion.132
  680.4 6.3 fusion.132
  692.8 6.3 fusion.132
  705.1 6.3 fusion.132
  713.9 6.6 convolution_convert_fusion
  721.1 51.5 %reduce-scatter.8.cloned.1.call-done = bf16[512,512]{1,0:T(8,128)(2,1)} async-done(((bf16[512,4096]{1,0:T(8,128)(2,1)}), bf16[512,512]{1,0:T(8,128)(2,1)}) %reduce-scatter.8.cloned.1.call-update) | async-done | bytes 524304 | tf_op jit(solution)/shard_map/reduce_scatter | solution.py:214
  (308 shorter events, 191.6 us)
Async XLA Ops:
  7.2 195.7 %copy-start = (bf16[512,1536]{1,0:T(8,128)(2,1)S(1)}, bf16[512,1536]{1,0:T(8,128)(2,1)}, u32[]{:S(2)}) copy-start(bf16[512,1536]{1,0:T(8,128)(2,1)} %param.18) | copy-start | bytes 4718596
  7.2 49.4 %all-gather.9.cloned.1.call-start = ((), (), s32[]{:S(2)}) async-start(), calls=%async_computation.3 | async-start | bytes 3538944 | tf_op jit(solution)/shard_map/all_gather | solution.py:163
  10.4 139.3 %reduce-scatter.4.cloned.1.call-start = ((), (), s32[]{:S(2)}) async-start(), calls=%async_computation.4 | async-start | bytes 3538944 | tf_op jit(solution)/shard_map/reduce_scatter | solution.py:166
  62.3 12.7 %collective-permute-start = (bf16[2,512,192]{1,2,0:T(8,128)(2,1)S(1)}, bf16[2,512,192]{1,2,0:T(8,128)(2,1)S(1)}, u32[]{:S(2)}, u32[]{:S(2)}) collective-permute-start(bf16[2,512,192]{1,2,0:T(8,128)(2,1)S(1)} %pad_maximum_fusion.2), channel_id=1, source_target_pairs={{0,8},{8,16},{16,24},{24,32},{32,40},{40,48},{48,56},{56,64},{64,7... | collective-permute-start | bytes 1179656 | tf_op jit(solution)/shard_map/ppermute | solution.py:16
  102.4 47.4 %copy-start.3 = (bf16[128,1536]{1,0:T(8,128)(2,1)S(1)}, bf16[128,1536]{1,0:T(8,128)(2,1)}, u32[]{:S(2)}) copy-start(bf16[128,1536]{1,0:T(8,128)(2,1)} %param.13) | copy-start | bytes 1179652
  106.2 90.8 %all-gather.11.cloned.1.call-start = ((), (), s32[]{:S(2)}) async-start(), calls=%async_computation.5 | async-start | bytes 3538944 | tf_op jit(solution)/shard_map/all_gather | solution.py:171
  152.9 104.5 %reduce-scatter.6.cloned.1.call-start = ((), (), s32[]{:S(2)}) async-start(), calls=%async_computation.6 | async-start | bytes 3538944 | tf_op jit(solution)/shard_map/reduce_scatter | solution.py:176
  202.9 54.5 %copy-start.5 = (bf16[128,1536]{1,0:T(8,128)(2,1)S(1)}, bf16[128,1536]{1,0:T(8,128)(2,1)}, u32[]{:S(2)}) copy-start(bf16[128,1536]{1,0:T(8,128)(2,1)} %reduce-scatter.4.cloned.1.call-done) | copy-start | bytes 1179652
  211.6 47.8 %copy-start.7 = (s32[128]{0:T(128)S(1)}, s32[128]{0:T(128)}, u32[]{:S(2)}) copy-start(s32[128]{0:T(128)} %param.14) | copy-start | bytes 1540
  211.6 92.1 %all-gather.13.cloned.1.call-start = ((), (), s32[]{:S(2)}) async-start(), calls=%async_computation.7 | async-start | bytes 3538944 | tf_op jit(solution)/shard_map/all_gather | solution.py:181
  259.3 102.7 %all-gather.15.cloned.1.call-start = ((), (), s32[]{:S(2)}) async-start(), calls=%async_computation.8 | async-start | bytes 4718592 | tf_op jit(solution)/shard_map/all_gather | solution.py:185
  309.4 132.2 %all-gather.19.cloned.1.call-start = ((), (), s32[]{:S(2)}) async-start(), calls=%async_computation.10 | async-start | bytes 8912896 | tf_op jit(solution)/shard_map/all_gather | solution.py:203
  370.9 144.0 %all-gather.17.cloned.1.call-start = ((), (), s32[]{:S(2)}) async-start(), calls=%async_computation.9 | async-start | bytes 8912896 | tf_op jit(solution)/shard_map/all_gather | solution.py:202
  377.6 395.1 %reduce-scatter.8.cloned.1.call-start = ((), (), s32[]{:S(2)}) async-start(), calls=%async_computation.11 | async-start | bytes 4718592 | tf_op jit(solution)/shard_map/reduce_scatter | solution.py:214
  519.9 6.0 copy-start.2
  531.9 6.3 copy-start.2
  544.3 6.3 copy-start.2
  556.7 6.3 copy-start.2
  569.0 6.3 copy-start.2
  581.4 6.3 copy-start.2
  593.8 6.3 copy-start.2
  606.2 6.3 copy-start.2
  618.5 6.3 copy-start.2
  630.9 6.3 copy-start.2
  643.3 6.3 copy-start.2
  655.6 6.3 copy-start.2
  668.0 6.3 copy-start.2
  680.4 6.3 copy-start.2
  692.8 6.3 copy-start.2
  705.1 6.3 copy-start.2
  713.8 60.8 %copy-start.1 = (bf16[512,1536]{1,0:T(8,128)(2,1)S(1)}, bf16[512,1536]{1,0:T(8,128)(2,1)}, u32[]{:S(2)}) copy-start(bf16[512,1536]{1,0:T(8,128)(2,1)} %param.18) | copy-start | bytes 4718596
  720.5 52.2 %copy-start.6 = (bf16[512,512]{1,0:T(8,128)(2,1)S(1)}, bf16[512,512]{1,0:T(8,128)(2,1)}, u32[]{:S(2)}) copy-start(bf16[512,512]{1,0:T(8,128)(2,1)} %convolution_convert_fusion.4) | copy-start | bytes 1572868
  (2 other events, 6.8 us)
Sparse Core Ops, SparseCore 0:
  10.5 46.0 all-gather.8
  106.3 43.4 reduce-scatter.3
  153.0 43.9 all-gather.10
  211.7 45.6 reduce-scatter.5
  259.5 44.1 all-gather.12
  309.6 52.4 all-gather.14
  371.0 70.6 all-gather.18
  444.2 70.6 all-gather.16
  720.6 51.9 reduce-scatter.7
where the time goes:
time: 784 us; the launch traced here: 781 us
  waiting for transfers between devices  414 us (53%)
  matrix products  222 us (28%)
  local copies, waits for them, and re-layouts  45.1 us (6%)
  other arithmetic  40.8 us (5%)
  blocking collectives  40.2 us (5%)
  between operations  14 us (2%)
    dot_general x16, matrix products, absorb(): jnp.einsum('hqk,khd->qhd', weights, value_floats, precision=lax.Precision...  99.9 us
    all_gather x1, waiting for transfers between devices, per_device(): lax.all_gather(keys_two, 'seq', axis=0, tiled=True)  73.2 us
    all_gather x1, waiting for transfers between devices, per_device(): wide = lax.all_gather(wide_cols, 'blk', axis=1, tiled=True)  52.5 us
    reduce_scatter x1, waiting for transfers between devices, per_device(): lax.psum_scatter(out_partial.astype(jnp.bfloat16), 'blk', scatter_dimensi...  51.5 us
    dot_general x16, matrix products, absorb(): jnp.einsum('qhd,khd->hqk', query_heads, key_block.reshape(key_count, head...  46.8 us
    all_gather x1, waiting for transfers between devices, per_device(): whole_normed = lax.all_gather(normed, 'blk', axis=0, tiled=True)  46.1 us
    reduce_scatter x1, waiting for transfers between devices, per_device(): lax.psum_scatter(mlp_partial.astype(jnp.bfloat16), 'blk', scatter_dimensi...  45.8 us
    reduce_scatter x1, waiting for transfers between devices, per_device(): lax.psum_scatter(attn_partial.astype(jnp.bfloat16), 'blk', scatter_dimens...  43.5 us
  transfers between devices with their start and end apart: 10, of which 10 were waited for; matrix products, arithmetic and copies ran while one was open for 4% of the time, Pallas kernels for 0%

commit v1 on v0

v1 whole, which is shorter than its diff:
```python
import jax
import jax.numpy as jnp
from jax import lax
from jax.experimental import pallas as pl
from jax.experimental.pallas import tpu as pltpu
from jax.sharding import PartitionSpec as P

D1 = 1536
H1 = 24
D2 = 4096
H2 = 32
WIN = 512
EXT = 16
BF16 = jnp.bfloat16
F32 = jnp.float32
MASKED = -1e30

PLACES = ((0, 0), (1, 0), (0, 1), (0, 3), (0, 2), (1, 2), (1, 1), (1, 3))


def flip_x(value):
    return lax.ppermute(value, "blk", [(i, i ^ 4) for i in range(8)])


def turn_z(value, steps):
    return lax.ppermute(value, "blk", [(i, (i & 4) | ((i + steps) & 3)) for i in range(8)])


def gather_blk(own):
    count = own.shape[0]
    across = flip_x(own)
    behind = turn_z(own, 1)
    ahead = turn_z(own, 3)
    near = jnp.concatenate([own, across, ahead, behind], axis=0)
    opposite = turn_z(near[: 2 * count], 2)
    diagonal = flip_x(near[2 * count :])
    far = jnp.concatenate([opposite, diagonal], axis=0)
    return near, far


def reduce_blk(near, far):
    count = near.shape[0] // 4
    opposite = turn_z(far[: 2 * count], 2)
    diagonal = flip_x(far[2 * count :])

    def plus(block, other):
        return near[block * count : (block + 1) * count].astype(F32) + other.astype(F32)

    across = flip_x(plus(1, opposite[count:]).astype(BF16))
    behind = turn_z(plus(2, diagonal[:count]).astype(BF16), 1)
    ahead = turn_z(plus(3, diagonal[count:]).astype(BF16), 3)
    return (
        plus(0, opposite[:count])
        + across.astype(F32)
        + behind.astype(F32)
        + ahead.astype(F32)
    )


def normalize(values):
    floats = values.astype(F32)
    return floats * lax.rsqrt(jnp.mean(floats * floats, axis=-1, keepdims=True) + 1e-06)


def dot(left, right):
    return jnp.dot(left, right, preferred_element_type=F32)


def window_kernel(info, qkv, halo, out):
    rows, width, size, stride = 128, D1 // 8, D1 // H1, 128 + EXT
    key_count = WIN + rows
    i = lax.broadcasted_iota(jnp.int32, (rows, key_count), 0)
    j = lax.broadcasted_iota(jnp.int32, (rows, key_count), 1)
    band = (j > i) & (j <= i + WIN)
    seq_position = info[8]
    for n in range(8):
        place = info[n]
        keys, values = [], []
        for k in range(n - 4, n + 1):
            if k >= 0:
                start = pl.multiple_of(info[k] * stride, 16)
                block = qkv[pl.ds(start, rows), :]
                keys.append(block[:, width : 2 * width])
                values.append(block[:, 2 * width :])
            else:
                block = halo[(k + 4) * rows : (k + 5) * rows, :]
                keys.append(block[:, :width])
                values.append(block[:, width:])
        keys = jnp.concatenate(keys, axis=0)
        values = jnp.concatenate(values, axis=0)
        queries = qkv[pl.ds(pl.multiple_of(place * stride, 16), rows), :width]
        allowed = band
        if n < 4:
            allowed = band & (j + ((n - 4) * rows + seq_position * 1024) >= 0)
        parts = []
        for h in range(width // size):
            cut = slice(h * size, (h + 1) * size)
            scores = lax.dot_general(
                queries[:, cut], keys[:, cut], (((1,), (1,)), ((), ())),
                preferred_element_type=F32,
            ) * size ** (-0.5)
            scores = jnp.where(allowed, scores, MASKED)
            largest = jnp.max(scores, axis=-1, keepdims=True)
            weights = jnp.exp(scores - largest)
            total = jnp.sum(weights, axis=-1, keepdims=True)
            parts.append(dot(weights.astype(BF16), values[:, cut]) / total)
        out[pl.ds(pl.multiple_of(place * rows, 16), rows), :] = jnp.concatenate(
            parts, axis=1
        ).astype(BF16)


def window_attend(info, qkv, halo):
    vmem = pl.BlockSpec(memory_space=pltpu.VMEM)
    return pl.pallas_call(
        window_kernel,
        out_shape=jax.ShapeDtypeStruct((1024, D1 // 8), BF16),
        in_specs=[pl.BlockSpec(memory_space=pltpu.SMEM), vmem, vmem],
        out_specs=vmem,
        compiler_params=pltpu.CompilerParams(vmem_limit_bytes=40 * 2**20),
        cost_estimate=pl.CostEstimate(
            flops=24 * 128 * 640 * 256, bytes_accessed=2 * 2**20, transcendentals=24 * 128 * 640
        ),
        name="window_attend",
    )(info, qkv, halo)


def project_kernel(info, wide_near, wide_far, weights, out, total, scale):
    step = pl.program_id(0)

    @pl.when(step == 0)
    def _():
        squares = jnp.zeros((512, 1), F32)
        for source in (wide_near, wide_far):
            for k in range(4):
                block = source[k * 512 : (k + 1) * 512, :].astype(F32)
                squares += jnp.sum(block * block, axis=-1, keepdims=True)
        scale[...] = jnp.broadcast_to(lax.rsqrt(squares / D2 + 1e-06), scale.shape)
        total[...] = jnp.zeros_like(total)

    def absorb(source, k):
        start = pl.multiple_of(k * 512, 512)
        block = source[pl.ds(start, 512), :].astype(F32) * scale[:, :1]
        total[...] += dot(block.astype(BF16), weights[...])

    @pl.when(step < 4)
    def _():
        absorb(wide_near, step)

    @pl.when(step >= 4)
    def _():
        absorb(wide_far, step - 4)

    @pl.when(step == 7)
    def _():
        out[...] = total[...].astype(BF16)


def project_two(block_of, wide_near, wide_far, weights):
    return pl.pallas_call(
        project_kernel,
        out_shape=jax.ShapeDtypeStruct((512, 1536), BF16),
        grid_spec=pltpu.PrefetchScalarGridSpec(
            num_scalar_prefetch=1,
            grid=(8,),
            in_specs=[
                pl.BlockSpec((2048, 512), lambda s, info: (0, 0)),
                pl.BlockSpec((2048, 512), lambda s, info: (0, 0)),
                pl.BlockSpec((512, 1536), lambda s, info: (info[s], 0)),
            ],
            out_specs=pl.BlockSpec((512, 1536), lambda s, info: (0, 0)),
            scratch_shapes=[pltpu.VMEM((512, 1536), F32), pltpu.VMEM((512, 128), F32)],
        ),
        compiler_params=pltpu.CompilerParams(vmem_limit_bytes=48 * 2**20),
        cost_estimate=pl.CostEstimate(
            flops=2 * 512 * 4096 * 1536, bytes_accessed=18 * 2**20, transcendentals=512
        ),
        name="project_two",
    )(block_of, wide_near, wide_far, weights)


def causal_kernel(info, queries, kv, out):
    half, core, y = info[0], info[1], info[2]
    slot = pl.program_id(0)
    own_group = half * 8 + ((y + slot) & 3) * 2 + core
    factor = 128 ** (-0.5) * 1.4426950408889634
    parts, rows = 2, 256
    query = [queries[0, p * rows : (p + 1) * rows, :] for p in range(parts)]

    def tile(group, carry, diagonal):
        other_x = (group >> 3) ^ half
        other_core = (group & 1) ^ core
        offset = ((group >> 1) - y) & 3
        block = (other_core * 2 + other_x) * 4 + offset
        keys = kv[block, :512, :128]
        values = kv[block, :512, 128:]
        valid = kv[block, 512 : 512 + EXT, :128].astype(F32)
        bias = jnp.concatenate([(valid[p : p + 1] - 1.0) * 1e30 for p in range(4)], axis=1)
        result = []
        for p in range(parts):
            largest, total, sums = carry[p]
            scores = lax.dot_general(
                query[p], keys, (((1,), (1,)), ((), ())), preferred_element_type=F32
            ) * factor + bias
            if diagonal:
                i = lax.broadcasted_iota(jnp.int32, scores.shape, 0) + p * rows
                j = lax.broadcasted_iota(jnp.int32, scores.shape, 1)
                scores = jnp.where(j <= i, scores, MASKED)
            new_largest = jnp.maximum(largest, jnp.max(scores, axis=-1, keepdims=True))
            decay = jnp.exp2(largest - new_largest)
            weights = jnp.exp2(scores - new_largest)
            total = total * decay + jnp.sum(weights, axis=-1, keepdims=True)
            sums = sums * decay + dot(weights.astype(BF16), values)
            result.append((new_largest, total, sums))
        return tuple(result)

    first = tuple(
        (jnp.full((rows, 1), MASKED, F32), jnp.zeros((rows, 1), F32), jnp.zeros((rows, 128), F32))
        for _ in range(parts)
    )
    carry = lax.fori_loop(0, own_group, lambda g, c: tile(g, c, False), first)
    carry = tile(own_group, carry, True)
    for p in range(parts):
        _, total, sums = carry[p]
        out[0, p * rows : (p + 1) * rows, :] = (sums / total).astype(BF16)


def causal_attend(info, queries, kv):
    return pl.pallas_call(
        causal_kernel,
        out_shape=jax.ShapeDtypeStruct((4, 512, 128), BF16),
        grid_spec=pltpu.PrefetchScalarGridSpec(
            num_scalar_prefetch=1,
            grid=(4,),
            in_specs=[
                pl.BlockSpec((1, 512, 128), lambda s, info: (s, 0, 0)),
                pl.BlockSpec((16, 512 + EXT, 256), lambda s, info: (0, 0, 0)),
            ],
            out_specs=pl.BlockSpec((1, 512, 128), lambda s, info: (s, 0, 0)),
        ),
        compiler_params=pltpu.CompilerParams(vmem_limit_bytes=48 * 2**20),
        cost_estimate=pl.CostEstimate(
            flops=36 * 512 * 512 * 512, bytes_accessed=6 * 2**20, transcendentals=36 * 2**18
        ),
        name="causal_attend",
    )(info, queries, kv)


def turn_y(value, steps):
    return lax.ppermute(
        value, "seq", [(i, (i & 9) | ((i + 2 * steps) & 6)) for i in range(16)]
    )


def flip_seq(value, bit):
    return lax.ppermute(value, "seq", [(i, i ^ bit) for i in range(16)])


def per_device(
    tokens, boundary, heads_in, heads_out, gate_up, down_weight, widen, heads_in_two, heads_out_two
):
    seq_position = lax.axis_index("seq")
    me = lax.axis_index("blk")
    rows = tokens.shape[0]
    capacity = 512
    width = D1 // 8
    block_of = jnp.stack([((me ^ (4 * x)) & 4) | ((me + z) & 3) for x, z in PLACES])
    numbers = jnp.arange(8, dtype=jnp.int32)
    place_of = jnp.sum(
        jnp.where(block_of[None, :] == numbers[:, None], numbers[None, :], 0), axis=1
    )

    heads_in_flat, gate_flat, up_flat, heads_two_flat = lax.optimization_barrier(
        (
            heads_in.reshape(D1, 3 * width),
            gate_up[:, 0, :],
            gate_up[:, 1, :],
            heads_in_two.reshape(D2, 1536),
        )
    )

    normed = normalize(tokens).astype(BF16)
    marks_row = jnp.pad(boundary.astype(BF16)[None, :], ((0, EXT - 1), (0, D1 - rows)))
    near, far = gather_blk(jnp.concatenate([normed, marks_row], axis=0))
    marks = jnp.concatenate([near, far], axis=0).reshape(8, rows + EXT, D1)[:, rows, :rows]
    qkv = jnp.concatenate(
        [dot(near, heads_in_flat).astype(BF16), dot(far, heads_in_flat).astype(BF16)], axis=0
    )
    edge = jnp.concatenate(
        [
            lax.dynamic_slice(qkv, (place_of[n] * (rows + EXT), width), (rows, 2 * width))
            for n in range(4, 8)
        ],
        axis=0,
    )
    halo = lax.ppermute(edge, "seq", [(i, i + 1) for i in range(15)])
    info = jnp.concatenate([place_of, seq_position[None]]).astype(jnp.int32)
    attended = window_attend(info, qkv, halo)
    attn_near = dot(attended[: 4 * rows], heads_out).astype(BF16)
    attn_far = dot(attended[4 * rows :], heads_out).astype(BF16)
    mid_stream = (tokens.astype(F32) + reduce_blk(attn_near, attn_far)).astype(BF16)

    normed_mid = normalize(mid_stream).astype(BF16)

    def mlp(block):
        hidden = jax.nn.silu(dot(block, gate_flat)) * dot(block, up_flat)
        return dot(hidden.astype(BF16), down_weight).astype(BF16)

    near, far = gather_blk(normed_mid)
    mlp_near, mlp_far = mlp(near), mlp(far)
    level_one = (mid_stream.astype(F32) + reduce_blk(mlp_near, mlp_far)).astype(BF16)

    marks = marks.astype(F32)
    counts = jnp.sum(marks, axis=1)
    before = jnp.sum(
        jnp.where(block_of[None, :] < block_of[:, None], counts[None, :], 0.0), axis=1
    )
    steps = jnp.arange(rows)
    running = dot(marks.astype(BF16), (steps[:, None] <= steps[None, :]).astype(BF16))
    slots = jnp.where(marks > 0.5, before[:, None] + running - 1.0, -1.0).astype(jnp.int32)
    span_count = jnp.sum(counts).astype(jnp.int32)
    selector = (
        slots.reshape(1, 8 * rows) == jnp.arange(capacity, dtype=jnp.int32)[:, None]
    ).astype(BF16)
    near, far = gather_blk(level_one)
    pooled = (dot(selector[:, : 4 * rows], near) + dot(selector[:, 4 * rows :], far)).astype(BF16)
    wide_cols = dot(pooled, widen).astype(BF16)

    wide_near, wide_far = gather_blk(wide_cols)
    qkv_two = project_two(block_of.astype(jnp.int32), wide_near, wide_far, heads_two_flat)
    validity = (jnp.arange(capacity, dtype=jnp.int32) < span_count).astype(F32)
    valid_rows = jnp.pad(
        validity.reshape(4, 128).astype(BF16), ((0, EXT - 4), (0, 0))
    )
    zero_rows = jnp.zeros((EXT, 128), BF16)
    core, y, half = seq_position & 1, (seq_position >> 1) & 3, seq_position >> 3

    def chunk(offset):
        head = (y + offset) & 3
        parts = [
            lax.dynamic_slice(qkv_two, (0, (4 * i + head) * 128), (capacity, 128))
            for i in range(3)
        ]
        parts = [
            jnp.concatenate([part, extra], axis=0)
            for part, extra in zip(parts, (zero_rows, valid_rows, zero_rows), strict=True)
        ]
        return jnp.concatenate(parts, axis=1)

    from_behind = turn_y(chunk(1), 1)
    from_ahead = turn_y(chunk(3), 3)
    from_opposite = turn_y(chunk(2), 2)
    mine = jnp.stack([chunk(0), from_ahead, from_opposite, from_behind])
    own_kv = mine[:, :, 128:]
    kv_pair = jnp.stack([own_kv, flip_seq(own_kv, 8)])
    kv_all = jnp.stack([kv_pair, flip_seq(kv_pair, 1)]).reshape(16, capacity + EXT, 256)
    info_two = jnp.stack([half, core, y]).astype(jnp.int32)
    mixed = causal_attend(info_two, mine[:, :capacity, :128], kv_all)
    back = [mixed[0], turn_y(mixed[3], 3), turn_y(mixed[2], 2), turn_y(mixed[1], 1)]
    heads = jnp.concatenate([back[0], back[1], back[2], back[3]] * 2, axis=1)
    attended_two = lax.dynamic_slice(heads, (0, ((4 - y) & 3) * 128), (capacity, 512))

    def columns(place):
        part = lax.dynamic_slice(heads_out_two, (0, block_of[place] * 512), (512, 512))
        return dot(attended_two, part).astype(BF16)

    out_far = jnp.concatenate([columns(place) for place in range(4, 8)], axis=0)
    out_near = jnp.concatenate([columns(place) for place in range(4)], axis=0)
    level_two = (
        (wide_cols.astype(F32) + reduce_blk(out_near, out_far)) * validity[:, None]
    ).astype(BF16)
    return (level_one, level_two)


def solution(mesh):
    placed = (
        P(("seq", "blk"), None),
        P(("seq", "blk")),
        P(None, None, "blk"),
        P("blk", None),
        P(None, None, "blk"),
        P("blk", None),
        P(None, "blk"),
        P(None, None, "blk"),
        P("blk", None),
    )
    return jax.shard_map(
        per_device,
        mesh=mesh,
        in_specs=placed,
        out_specs=(P(("seq", "blk"), None), P("seq", "blk")),
        check_vma=False,
    )
```

time: 784 us -> 455 us (0.58)
  waiting for transfers between devices: 414 us -> 192 us
  matrix products: 222 us -> 39.5 us
  starting transfers between devices: 2.47 us -> 75.2 us
  Pallas kernels: 0 us -> 63.5 us
  blocking collectives: 40.2 us -> 0 us
  other arithmetic: 40.8 us -> 21.7 us
  between operations: 14 us -> 4.5 us
    all_gather x6 -> x0, waiting for transfers between devices: 266 us -> none  [the longest x1 73.2 us: per_device(): lax.all_gather(keys_two, 'seq', axis=0, tiled=True)]
    ppermute x1 -> x44, waiting for transfers between devices: 6.84 us -> 192 us  [the longest x21 96.8 us: turn_z(): lax.ppermute(value, 'blk', [(i, i & 4 | i + steps & 3) for i in range(8)])]
    dot_general x45 -> x19, matrix products: 211 us -> 39.5 us  [dot(): return jnp.dot(left, right, preferred_element_type=F32)]
    reduce_scatter x3 -> x0, waiting for transfers between devices: 141 us -> none  [the longest x1 51.5 us: per_device(): lax.psum_scatter(out_partial.astype(jnp.bfloat16), 'blk', scatter_dimensi...]
    ppermute x1 -> x44, starting transfers between devices: 1.92 us -> 75.2 us  [the longest x21 35 us: turn_z(): lax.ppermute(value, 'blk', [(i, i & 4 | i + steps & 3) for i in range(8)])]
    pallas_call x0 -> x3, Pallas kernels: none -> 63.5 us  [the longest x1 41.8 us: causal_attend(): pl.pallas_call(causal_kernel, out_shape=jax.ShapeDtypeStruct((4, 512, 128...]
    all_gather x2 -> x0, blocking collectives: 40.2 us -> none  [the longest x1 22.7 us: per_device(): lax.all_gather(validity.astype(jnp.bfloat16), 'seq', axis=0, tiled=True)]
    dynamic_slice x54 -> x1, local copies, waits for them, and re-layouts: 32.3 us -> 0.33 us  [chunk(): lax.dynamic_slice(qkv_two, (0, (4 * i + head) * 128), (capacity, 128))]
  transfers between devices with their start and end apart: 10 -> 44, of which waited for: 10 -> 32; matrix products, arithmetic and copies ran while one was open for 4% -> 15% of each run, Pallas kernels for 0% -> 0%
where the time goes in v1:
time: 455 us; the launch traced here: 448 us
  waiting for transfers between devices  192 us (42%)
  starting transfers between devices  75.2 us (17%)
  Pallas kernels  63.5 us (14%)
  local copies, waits for them, and re-layouts  51.6 us (11%)
  matrix products  39.5 us (9%)
  other arithmetic  21.7 us (5%)
    ppermute x21, waiting for transfers between devices, turn_z(): lax.ppermute(value, 'blk', [(i, i & 4 | i + steps & 3) for i in range(8)])  96.8 us
    ppermute x14, waiting for transfers between devices, flip_x(): return lax.ppermute(value, 'blk', [(i, i ^ 4) for i in range(8)])  48.3 us
    pallas_call x1, Pallas kernels, causal_attend(): pl.pallas_call(causal_kernel, out_shape=jax.ShapeDtypeStruct((4, 512, 128...  41.8 us
    dot_general x19, matrix products, dot(): return jnp.dot(left, right, preferred_element_type=F32)  39.5 us
    ppermute x21, starting transfers between devices, turn_z(): lax.ppermute(value, 'blk', [(i, i & 4 | i + steps & 3) for i in range(8)])  35 us
    unnamed x59, local copies, waits for them, and re-layouts  23.8 us
    ppermute x6, starting transfers between devices, turn_y(): lax.ppermute(value, 'seq', [(i, i & 9 | i + 2 * steps & 6) for i in range...  19.9 us
    ppermute x2, waiting for transfers between devices, flip_seq(): return lax.ppermute(value, 'seq', [(i, i ^ bit) for i in range(16)])  19.7 us
  transfers between devices with their start and end apart: 44, of which 32 were waited for; matrix products, arithmetic and copies ran while one was open for 15% of the time, Pallas kernels for 0%

profile of v1, /device:TPU:6, one launch (start us, length us, event | category | flops | bytes accessed | tf_op | source)
XLA Modules:
  0.0 447.9 jit_solution(6611964931971763867)
XLA Ops:
  7.0 4.0 collective-permute-start.1
  11.0 4.4 fusion.121
  21.4 16.9 %copy.24 = bf16[4096,3,512]{0,2,1:T(8,128)(2,1)} copy(bf16[4096,3,512]{2,0,1:T(8,128)(2,1)} %param.16) | data formatting | bytes 25165824 | tf_op args[7]
  47.7 13.1 %collective-permute-done.3 = bf16[288,1536]{1,0:T(8,128)(2,1)S(1)} collective-permute-done((bf16[288,1536]{1,0:T(8,128)(2,1)S(1)}, bf16[288,1536]{1,0:T(8,128)(2,1)S(1)}, u32[]{:S(2)}, u32[]{:S(2)}) %collective-permute-start.3) | collective-permute-done | bytes 884768 | tf_op jit(solution)/shard_map/ppermute | solution.py:26
  65.8 10.4 %collective-permute-done.5.halo = bf16[512,384]{1,0:T(8,128)(2,1)S(1)} collective-permute-done((bf16[512,384]{1,0:T(8,128)(2,1)S(1)}, bf16[512,384]{1,0:T(8,128)(2,1)S(1)}, u32[]{:S(2)}, u32[]{:S(2)}) %collective-permute-start.5) | collective-permute-done | bytes 393248 | tf_op jit(solution)/shard_map/ppermute | solution.py:295
  76.1 8.9 %window_attend.1 = bf16[1024,192]{1,0:T(8,128)(2,1)S(1)} custom-call(s32[9]{0:T(128)S(1)} %pad_add_fusion.info, bf16[1152,576]{1,0:T(8,128)(2,1)S(1)} %pad_maximum_fusion.1.qkv, bf16[512,384]{1,0:T(8,128)(2,1)S(1)} %collective-permute-done.5.halo), custom_call_target="tpu_custom_call" | custom-call | flops 503316480 | bytes 2097152 | tf_op jit(solution)/shard_map/window_attend/pallas_call | solution.py:114
  89.4 12.9 %collective-permute-done.6 = bf16[256,1536]{1,0:T(8,128)(2,1)S(1)} collective-permute-done((bf16[256,1536]{1,0:T(8,128)(2,1)S(1)}, bf16[256,1536]{1,0:T(8,128)(2,1)S(1)}, u32[]{:S(2)}, u32[]{:S(2)}) %collective-permute-start.6) | collective-permute-done | bytes 786464 | tf_op jit(solution)/shard_map/ppermute | solution.py:26
  102.7 5.3 %collective-permute-start.10 = (bf16[128,1536]{1,0:T(8,128)(2,1)S(1)}, bf16[128,1536]{1,0:T(8,128)(2,1)S(1)}, u32[]{:S(2)}, u32[]{:S(2)}) collective-permute-start(bf16[128,1536]{1,0:T(8,128)(2,1)S(1)} %get-tuple-element.21), channel_id=1, source_target_pairs={{0,3},{1,0},{2,1},{3,2},{4,7},{5,4},{6,5},{7,6},{8,11},{9,8},{10,9... | collective-permute-start | bytes 1179656 | tf_op jit(solution)/shard_map/ppermute | solution.py:26
  109.2 5.9 %collective-permute-done.10 = bf16[128,1536]{1,0:T(8,128)(2,1)S(1)} collective-permute-done((bf16[128,1536]{1,0:T(8,128)(2,1)S(1)}, bf16[128,1536]{1,0:T(8,128)(2,1)S(1)}, u32[]{:S(2)}, u32[]{:S(2)}) %collective-permute-start.10) | collective-permute-done | bytes 393248 | tf_op jit(solution)/shard_map/ppermute | solution.py:26
  115.1 4.5 %collective-permute-done.7 = bf16[128,1536]{1,0:T(8,128)(2,1)S(1)} collective-permute-done((bf16[128,1536]{1,0:T(8,128)(2,1)S(1)}, bf16[128,1536]{1,0:T(8,128)(2,1)S(1)}, u32[]{:S(2)}, u32[]{:S(2)}) %collective-permute-start.7) | collective-permute-done | bytes 393248 | tf_op jit(solution)/shard_map/ppermute | solution.py:22
  125.1 9.0 %collective-permute-done.11 = bf16[128,1536]{1,0:T(8,128)(2,1)S(1)} collective-permute-done((bf16[128,1536]{1,0:T(8,128)(2,1)S(1)}, bf16[128,1536]{1,0:T(8,128)(2,1)S(1)}, u32[]{:S(2)}, u32[]{:S(2)}) %collective-permute-start.11) | collective-permute-done | bytes 393248 | tf_op jit(solution)/shard_map/ppermute | solution.py:22
  139.7 8.8 %collective-permute-done.14 = bf16[256,1536]{1,0:T(8,128)(2,1)S(1)} collective-permute-done((bf16[256,1536]{1,0:T(8,128)(2,1)S(1)}, bf16[256,1536]{1,0:T(8,128)(2,1)S(1)}, u32[]{:S(2)}, u32[]{:S(2)}) %collective-permute-start.14) | collective-permute-done | bytes 786464 | tf_op jit(solution)/shard_map/ppermute | solution.py:26
  154.0 5.7 %convolution_convert_fusion = bf16[512,1536]{1,0:T(8,128)(2,1)} fusion(bf16[512,1536]{1,0:T(8,128)(2,1)} %param.14, f32[512,512]{1,0:T(8,128)} %fusion.127, bf16[512,1536]{1,0:T(8,128)(2,1)} %copy-done.13, bf16[1536,512]{1,0:T(8,128)(2,1)} %get-tuple-element.8), kind=kOutput, calls=%fused_computation.2 | convolution fusion | flops 1612972032 | bytes 7340032 | tf_op jit(solution)/shard_map/dot_general | solution.py:66
  165.6 5.2 %convolution_convert_fusion.1 = bf16[512,1536]{1,0:T(8,128)(2,1)} fusion(bf16[512,1536]{1,0:T(8,128)(2,1)} %param.14, f32[512,512]{1,0:T(8,128)} %fusion.82, bf16[1536,512]{1,0:T(8,128)(2,1)S(1)} %copy-done.5, bf16[128,1536]{1,0:T(8,128)(2,1)} %copy-done.18, bf16[128,1536]{1,0:T(8,128)(2,1)} %copy-done.16, bf16[128,1536]{1,0:T(8,128)(2,1)} %copy-done.14, ...), kind=kOutput, calls=%fused_computation.3 | convolution fusion | flops 1619263488 | bytes 7340032 | tf_op jit(solution)/shard_map/dot_general | solution.py:66
  170.8 9.5 %collective-permute-done.16 = bf16[256,1536]{1,0:T(8,128)(2,1)} collective-permute-done((bf16[256,1536]{1,0:T(8,128)(2,1)}, bf16[256,1536]{1,0:T(8,128)(2,1)}, u32[]{:S(2)}, u32[]{:S(2)}) %collective-permute-start.16) | collective-permute-done | bytes 786464 | tf_op jit(solution)/shard_map/ppermute | solution.py:26
  186.5 6.9 %collective-permute-done.17 = bf16[128,1536]{1,0:T(8,128)(2,1)S(1)} collective-permute-done((bf16[128,1536]{1,0:T(8,128)(2,1)S(1)}, bf16[128,1536]{1,0:T(8,128)(2,1)S(1)}, u32[]{:S(2)}, u32[]{:S(2)}) %collective-permute-start.17) | collective-permute-done | bytes 393248 | tf_op jit(solution)/shard_map/ppermute | solution.py:22
  199.9 8.9 %collective-permute-done.21 = bf16[128,1536]{1,0:T(8,128)(2,1)S(1)} collective-permute-done((bf16[128,1536]{1,0:T(8,128)(2,1)S(1)}, bf16[128,1536]{1,0:T(8,128)(2,1)S(1)}, u32[]{:S(2)}, u32[]{:S(2)}) %collective-permute-start.21) | collective-permute-done | bytes 393248 | tf_op jit(solution)/shard_map/ppermute | solution.py:22
  212.4 11.3 %collective-permute-done.24 = bf16[256,1536]{1,0:T(8,128)(2,1)S(1)} collective-permute-done((bf16[256,1536]{1,0:T(8,128)(2,1)S(1)}, bf16[256,1536]{1,0:T(8,128)(2,1)S(1)}, u32[]{:S(2)}, u32[]{:S(2)}) %collective-permute-start.24) | collective-permute-done | bytes 786464 | tf_op jit(solution)/shard_map/ppermute | solution.py:26
  227.3 4.3 convolution_convert_fusion.13
  235.5 11.0 %collective-permute-done.26 = bf16[512,512]{1,0:T(8,128)(2,1)S(1)} collective-permute-done((bf16[512,512]{1,0:T(8,128)(2,1)S(1)}, bf16[512,512]{1,0:T(8,128)(2,1)S(1)}, u32[]{:S(2)}, u32[]{:S(2)}) %collective-permute-start.26) | collective-permute-done | bytes 524320 | tf_op jit(solution)/shard_map/ppermute | solution.py:22
  253.0 16.7 %copy.28.weights = bf16[4096,1536]{1,0:T(8,128)(2,1)} copy(bf16[4096,1536]{0,1:T(8,128)(2,1)} %bitcast.78) | data formatting | bytes 25165824 | tf_op jit(solution)/shard_map/optimization_barrier | solution.py:272
  272.2 12.9 %project_two.1 = bf16[512,1536]{1,0:T(8,128)(2,1)S(1)} custom-call(s32[8]{0:T(128)S(1)} %stack.80.info, bf16[2048,512]{1,0:T(8,128)(2,1)S(1)} %pad_maximum_fusion.3.wide_near, bf16[2048,512]{1,0:T(8,128)(2,1)S(1)} %pad_maximum_fusion.4.wide_far, bf16[4096,1536]{1,0:T(8,128)(2,1)} %copy.28.weights), custom_call_target="tpu_custom_call" | custom-call | flops 6442450944 | bytes 18874368 | tf_op jit(solution)/shard_map/project_two/pallas_call | solution.py:159
  285.6 7.1 %collective-permute-start.31 = (bf16[528,384]{1,0:T(8,128)(2,1)S(1)}, bf16[528,384]{1,0:T(8,128)(2,1)S(1)}, u32[]{:S(2)}, u32[]{:S(2)}) collective-permute-start(bf16[528,384]{1,0:T(8,128)(2,1)S(1)} %get-tuple-element.56), channel_id=1, source_target_pairs={{0,48},{8,56},{16,0},{24,8},{32,16},{40,24},{48,32},{56,40},{64,11... | collective-permute-start | bytes 1216520 | tf_op jit(solution)/shard_map/ppermute | solution.py:249
  292.8 7.5 %collective-permute-start.32 = (bf16[528,384]{1,0:T(8,128)(2,1)S(1)}, bf16[528,384]{1,0:T(8,128)(2,1)S(1)}, u32[]{:S(2)}, u32[]{:S(2)}) collective-permute-start(bf16[528,384]{1,0:T(8,128)(2,1)S(1)} %get-tuple-element.57), channel_id=1, source_target_pairs={{0,32},{8,40},{16,48},{24,56},{32,0},{40,8},{48,16},{56,24},{64,96... | collective-permute-start | bytes 1216520 | tf_op jit(solution)/shard_map/ppermute | solution.py:249
  306.2 4.2 collective-permute-done.33
  312.0 15.3 %collective-permute-done.34 = bf16[4,528,256]{2,1,0:T(8,128)(2,1)S(1)} collective-permute-done((bf16[4,528,256]{2,1,0:T(8,128)(2,1)S(1)}, bf16[4,528,256]{2,1,0:T(8,128)(2,1)S(1)}, u32[]{:S(2)}, u32[]{:S(2)}) %collective-permute-start.34) | collective-permute-done | bytes 1081376 | tf_op jit(solution)/shard_map/ppermute | solution.py:255
  329.8 4.4 collective-permute-done.35
  336.9 41.8 %causal_attend.1 = bf16[4,512,128]{2,1,0:T(8,128)(2,1)S(1)} custom-call(s32[3]{0:T(128)S(1)} %pad_add_fusion.1.info, bf16[4,512,128]{2,1,0:T(8,128)(2,1)S(1)} %pad_maximum_fusion.19.queries, bf16[16,528,256]{2,1,0:T(8,128)(2,1)S(1)} %bitcast.77), custom_call_target="tpu_custom_call" | custom-call | flops 4831838208 | bytes 6291456 | tf_op jit(solution)/shard_map/causal_attend/pallas_call | solution.py:228
  385.9 4.7 %collective-permute-done.38 = bf16[512,128]{1,0:T(8,128)(2,1)S(1)} collective-permute-done((bf16[512,128]{1,0:T(8,128)(2,1)S(1)}, bf16[512,128]{1,0:T(8,128)(2,1)S(1)}, u32[]{:S(2)}, u32[]{:S(2)}) %collective-permute-start.38) | collective-permute-done | bytes 131104 | tf_op jit(solution)/shard_map/ppermute | solution.py:249
  400.1 20.5 %collective-permute-done.39 = bf16[1024,512]{1,0:T(8,128)(2,1)} collective-permute-done((bf16[1024,512]{1,0:T(8,128)(2,1)}, bf16[1024,512]{1,0:T(8,128)(2,1)}, u32[]{:S(2)}, u32[]{:S(2)}) %collective-permute-start.39) | collective-permute-done | bytes 1048608 | tf_op jit(solution)/shard_map/ppermute | solution.py:26
  432.5 4.7 %collective-permute-done.40 = bf16[512,512]{1,0:T(8,128)(2,1)} collective-permute-done((bf16[512,512]{1,0:T(8,128)(2,1)}, bf16[512,512]{1,0:T(8,128)(2,1)}, u32[]{:S(2)}, u32[]{:S(2)}) %collective-permute-start.40) | collective-permute-done | bytes 524320 | tf_op jit(solution)/shard_map/ppermute | solution.py:22
  437.2 5.0 %collective-permute-done.42 = bf16[512,512]{1,0:T(8,128)(2,1)} collective-permute-done((bf16[512,512]{1,0:T(8,128)(2,1)}, bf16[512,512]{1,0:T(8,128)(2,1)}, u32[]{:S(2)}, u32[]{:S(2)}) %collective-permute-start.42) | collective-permute-done | bytes 524320 | tf_op jit(solution)/shard_map/ppermute | solution.py:26
  (190 shorter events, 131.8 us)
Async XLA Ops:
  6.2 32.2 %collective-permute-start = (bf16[144,1536]{1,0:T(8,128)(2,1)}, bf16[144,1536]{1,0:T(8,128)(2,1)S(1)}, u32[]{:S(2)}, u32[]{:S(2)}) collective-permute-start(bf16[144,1536]{1,0:T(8,128)(2,1)} %pad_maximum_fusion.20), channel_id=1, source_target_pairs={{0,4},{1,5},{2,6},{3,7},{4,0},{5,1},{6,2},{7,3},{8,12},{9,13},{10,... | collective-permute-start | bytes 1327112 | tf_op jit(solution)/shard_map/ppermute | solution.py:22
  7.0 33.3 %collective-permute-start.1 = (bf16[144,1536]{1,0:T(8,128)(2,1)}, bf16[144,1536]{1,0:T(8,128)(2,1)S(1)}, u32[]{:S(2)}, u32[]{:S(2)}) collective-permute-start(bf16[144,1536]{1,0:T(8,128)(2,1)} %pad_maximum_fusion.20), channel_id=1, source_target_pairs={{0,3},{1,0},{2,1},{3,2},{4,7},{5,4},{6,5},{7,6},{8,11},{9,8},{10,9... | collective-permute-start | bytes 1327112 | tf_op jit(solution)/shard_map/ppermute | solution.py:26
  11.0 29.3 %collective-permute-start.2 = (bf16[144,1536]{1,0:T(8,128)(2,1)}, bf16[144,1536]{1,0:T(8,128)(2,1)S(1)}, u32[]{:S(2)}, u32[]{:S(2)}) collective-permute-start(bf16[144,1536]{1,0:T(8,128)(2,1)} %pad_maximum_fusion.20), channel_id=1, source_target_pairs={{0,1},{1,2},{2,3},{3,0},{4,5},{5,6},{6,7},{7,4},{8,9},{9,10},{10,1... | collective-permute-start | bytes 1327112 | tf_op jit(solution)/shard_map/ppermute | solution.py:26
  38.4 22.4 %collective-permute-start.3 = (bf16[288,1536]{1,0:T(8,128)(2,1)S(1)}, bf16[288,1536]{1,0:T(8,128)(2,1)S(1)}, u32[]{:S(2)}, u32[]{:S(2)}) collective-permute-start(bf16[288,1536]{1,0:T(8,128)(2,1)S(1)} %pad_maximum_fusion.13), channel_id=1, source_target_pairs={{0,2},{1,3},{2,0},{3,1},{4,6},{5,7},{6,4},{7,5},{8,10},{9,11},{10,... | collective-permute-start | bytes 2654216 | tf_op jit(solution)/shard_map/ppermute | solution.py:26
  40.4 20.4 %collective-permute-start.4 = (bf16[288,1536]{1,0:T(8,128)(2,1)S(1)}, bf16[288,1536]{1,0:T(8,128)(2,1)S(1)}, u32[]{:S(2)}, u32[]{:S(2)}) collective-permute-start(bf16[288,1536]{1,0:T(8,128)(2,1)S(1)} %pad_maximum_fusion.14), channel_id=1, source_target_pairs={{0,4},{1,5},{2,6},{3,7},{4,0},{5,1},{6,2},{7,3},{8,12},{9,13},{10,... | collective-permute-start | bytes 2654216 | tf_op jit(solution)/shard_map/ppermute | solution.py:22
  63.4 12.7 %collective-permute-start.5 = (bf16[512,384]{1,0:T(8,128)(2,1)S(1)}, bf16[512,384]{1,0:T(8,128)(2,1)S(1)}, u32[]{:S(2)}, u32[]{:S(2)}) collective-permute-start(bf16[512,384]{1,0:T(8,128)(2,1)S(1)} %pad_maximum_fusion.21), channel_id=1, source_target_pairs={{0,8},{8,16},{16,24},{24,32},{32,40},{40,48},{48,56},{56,64},{64,7... | collective-permute-start | bytes 1179656 | tf_op jit(solution)/shard_map/ppermute | solution.py:295
  85.7 16.6 %collective-permute-start.6 = (bf16[256,1536]{1,0:T(8,128)(2,1)S(1)}, bf16[256,1536]{1,0:T(8,128)(2,1)S(1)}, u32[]{:S(2)}, u32[]{:S(2)}) collective-permute-start(bf16[256,1536]{1,0:T(8,128)(2,1)S(1)} %get-tuple-element.40), channel_id=1, source_target_pairs={{0,2},{1,3},{2,0},{3,1},{4,6},{5,7},{6,4},{7,5},{8,10},{9,11},{10,... | collective-permute-start | bytes 2359304 | tf_op jit(solution)/shard_map/ppermute | solution.py:26
  87.7 14.8 %collective-permute-start.8 = (bf16[256,1536]{1,0:T(8,128)(2,1)S(1)}, bf16[256,1536]{1,0:T(8,128)(2,1)S(1)}, u32[]{:S(2)}, u32[]{:S(2)}) collective-permute-start(bf16[256,1536]{1,0:T(8,128)(2,1)S(1)} %get-tuple-element.41), channel_id=1, source_target_pairs={{0,4},{1,5},{2,6},{3,7},{4,0},{5,1},{6,2},{7,3},{8,12},{9,13},{10,... | collective-permute-start | bytes 2359304 | tf_op jit(solution)/shard_map/ppermute | solution.py:22
  102.7 12.4 %collective-permute-start.10 = (bf16[128,1536]{1,0:T(8,128)(2,1)S(1)}, bf16[128,1536]{1,0:T(8,128)(2,1)S(1)}, u32[]{:S(2)}, u32[]{:S(2)}) collective-permute-start(bf16[128,1536]{1,0:T(8,128)(2,1)S(1)} %get-tuple-element.21), channel_id=1, source_target_pairs={{0,3},{1,0},{2,1},{3,2},{4,7},{5,4},{6,5},{7,6},{8,11},{9,8},{10,9... | collective-permute-start | bytes 1179656 | tf_op jit(solution)/shard_map/ppermute | solution.py:26
  109.2 12.3 %collective-permute-start.9 = (bf16[128,1536]{1,0:T(8,128)(2,1)S(1)}, bf16[128,1536]{1,0:T(8,128)(2,1)S(1)}, u32[]{:S(2)}, u32[]{:S(2)}) collective-permute-start(bf16[128,1536]{1,0:T(8,128)(2,1)S(1)} %get-tuple-element.20), channel_id=1, source_target_pairs={{0,1},{1,2},{2,3},{3,0},{4,5},{5,6},{6,7},{7,4},{8,9},{9,10},{10,1... | collective-permute-start | bytes 1179656 | tf_op jit(solution)/shard_map/ppermute | solution.py:26
  123.1 12.1 %collective-permute-start.12 = (bf16[128,1536]{1,0:T(8,128)(2,1)S(1)}, bf16[128,1536]{1,0:T(8,128)(2,1)S(1)}, u32[]{:S(2)}, u32[]{:S(2)}) collective-permute-start(bf16[128,1536]{1,0:T(8,128)(2,1)S(1)} %fusion.61), channel_id=1, source_target_pairs={{0,3},{1,0},{2,1},{3,2},{4,7},{5,4},{6,5},{7,6},{8,11},{9,8},{10,9... | collective-permute-start | bytes 1179656 | tf_op jit(solution)/shard_map/ppermute | solution.py:26
  123.1 15.3 %collective-permute-start.13 = (bf16[128,1536]{1,0:T(8,128)(2,1)S(1)}, bf16[128,1536]{1,0:T(8,128)(2,1)S(1)}, u32[]{:S(2)}, u32[]{:S(2)}) collective-permute-start(bf16[128,1536]{1,0:T(8,128)(2,1)S(1)} %fusion.61), channel_id=1, source_target_pairs={{0,1},{1,2},{2,3},{3,0},{4,5},{5,6},{6,7},{7,4},{8,9},{9,10},{10,1... | collective-permute-start | bytes 1179656 | tf_op jit(solution)/shard_map/ppermute | solution.py:26
  135.0 13.6 %collective-permute-start.14 = (bf16[256,1536]{1,0:T(8,128)(2,1)S(1)}, bf16[256,1536]{1,0:T(8,128)(2,1)S(1)}, u32[]{:S(2)}, u32[]{:S(2)}) collective-permute-start(bf16[256,1536]{1,0:T(8,128)(2,1)S(1)} %pad_maximum_fusion.15), channel_id=1, source_target_pairs={{0,2},{1,3},{2,0},{3,1},{4,6},{5,7},{6,4},{7,5},{8,10},{9,11},{10,... | collective-permute-start | bytes 2359304 | tf_op jit(solution)/shard_map/ppermute | solution.py:26
  138.5 12.3 %collective-permute-start.15 = (bf16[256,1536]{1,0:T(8,128)(2,1)S(1)}, bf16[256,1536]{1,0:T(8,128)(2,1)S(1)}, u32[]{:S(2)}, u32[]{:S(2)}) collective-permute-start(bf16[256,1536]{1,0:T(8,128)(2,1)S(1)} %pad_maximum_fusion.16), channel_id=1, source_target_pairs={{0,4},{1,5},{2,6},{3,7},{4,0},{5,1},{6,2},{7,3},{8,12},{9,13},{10,... | collective-permute-start | bytes 2359304 | tf_op jit(solution)/shard_map/ppermute | solution.py:22
  162.5 17.8 %collective-permute-start.16 = (bf16[256,1536]{1,0:T(8,128)(2,1)}, bf16[256,1536]{1,0:T(8,128)(2,1)}, u32[]{:S(2)}, u32[]{:S(2)}) collective-permute-start(bf16[256,1536]{1,0:T(8,128)(2,1)} %get-tuple-element.37), channel_id=1, source_target_pairs={{0,2},{1,3},{2,0},{3,1},{4,6},{5,7},{6,4},{7,5},{8,10},{9,11},{10,... | collective-permute-start | bytes 2359304 | tf_op jit(solution)/shard_map/ppermute | solution.py:26
  162.7 17.6 %collective-permute-start.18 = (bf16[256,1536]{1,0:T(8,128)(2,1)}, bf16[256,1536]{1,0:T(8,128)(2,1)S(1)}, u32[]{:S(2)}, u32[]{:S(2)}) collective-permute-start(bf16[256,1536]{1,0:T(8,128)(2,1)} %get-tuple-element.38), channel_id=1, source_target_pairs={{0,4},{1,5},{2,6},{3,7},{4,0},{5,1},{6,2},{7,3},{8,12},{9,13},{10,... | collective-permute-start | bytes 2359304 | tf_op jit(solution)/shard_map/ppermute | solution.py:22
  196.7 12.1 %collective-permute-start.21 = (bf16[128,1536]{1,0:T(8,128)(2,1)S(1)}, bf16[128,1536]{1,0:T(8,128)(2,1)S(1)}, u32[]{:S(2)}, u32[]{:S(2)}) collective-permute-start(bf16[128,1536]{1,0:T(8,128)(2,1)S(1)} %fusion.62), channel_id=1, source_target_pairs={{0,4},{1,5},{2,6},{3,7},{4,0},{5,1},{6,2},{7,3},{8,12},{9,13},{10,... | collective-permute-start | bytes 1179656 | tf_op jit(solution)/shard_map/ppermute | solution.py:22
  208.9 14.8 %collective-permute-start.24 = (bf16[256,1536]{1,0:T(8,128)(2,1)S(1)}, bf16[256,1536]{1,0:T(8,128)(2,1)S(1)}, u32[]{:S(2)}, u32[]{:S(2)}) collective-permute-start(bf16[256,1536]{1,0:T(8,128)(2,1)S(1)} %pad_maximum_fusion.17), channel_id=1, source_target_pairs={{0,2},{1,3},{2,0},{3,1},{4,6},{5,7},{6,4},{7,5},{8,10},{9,11},{10,... | collective-permute-start | bytes 2359304 | tf_op jit(solution)/shard_map/ppermute | solution.py:26
  209.9 14.8 %collective-permute-start.25 = (bf16[256,1536]{1,0:T(8,128)(2,1)S(1)}, bf16[256,1536]{1,0:T(8,128)(2,1)S(1)}, u32[]{:S(2)}, u32[]{:S(2)}) collective-permute-start(bf16[256,1536]{1,0:T(8,128)(2,1)S(1)} %pad_maximum_fusion.18), channel_id=1, source_target_pairs={{0,4},{1,5},{2,6},{3,7},{4,0},{5,1},{6,2},{7,3},{8,12},{9,13},{10,... | collective-permute-start | bytes 2359304 | tf_op jit(solution)/shard_map/ppermute | solution.py:22
  231.6 14.9 %collective-permute-start.26 = (bf16[512,512]{1,0:T(8,128)(2,1)S(1)}, bf16[512,512]{1,0:T(8,128)(2,1)S(1)}, u32[]{:S(2)}, u32[]{:S(2)}) collective-permute-start(bf16[512,512]{1,0:T(8,128)(2,1)S(1)} %convolution_convert_fusion.13), channel_id=1, source_target_pairs={{0,4},{1,5},{2,6},{3,7},{4,0},{5,1},{6,2},{7,3},{8,12},{9,13},{10,... | collective-permute-start | bytes 1572872 | tf_op jit(solution)/shard_map/ppermute | solution.py:22
  232.5 18.0 %collective-permute-start.27 = (bf16[512,512]{1,0:T(8,128)(2,1)S(1)}, bf16[512,512]{1,0:T(8,128)(2,1)S(1)}, u32[]{:S(2)}, u32[]{:S(2)}) collective-permute-start(bf16[512,512]{1,0:T(8,128)(2,1)S(1)} %convolution_convert_fusion.13), channel_id=1, source_target_pairs={{0,3},{1,0},{2,1},{3,2},{4,7},{5,4},{6,5},{7,6},{8,11},{9,8},{10,9... | collective-permute-start | bytes 1572872 | tf_op jit(solution)/shard_map/ppermute | solution.py:26
  235.5 15.0 %collective-permute-start.28 = (bf16[512,512]{1,0:T(8,128)(2,1)S(1)}, bf16[512,512]{1,0:T(8,128)(2,1)S(1)}, u32[]{:S(2)}, u32[]{:S(2)}) collective-permute-start(bf16[512,512]{1,0:T(8,128)(2,1)S(1)} %convolution_convert_fusion.13), channel_id=1, source_target_pairs={{0,1},{1,2},{2,3},{3,0},{4,5},{5,6},{6,7},{7,4},{8,9},{9,10},{10,1... | collective-permute-start | bytes 1572872 | tf_op jit(solution)/shard_map/ppermute | solution.py:26
  246.6 23.9 %collective-permute-start.29 = (bf16[1024,512]{1,0:T(8,128)(2,1)S(1)}, bf16[1024,512]{1,0:T(8,128)(2,1)}, u32[]{:S(2)}, u32[]{:S(2)}) collective-permute-start(bf16[1024,512]{1,0:T(8,128)(2,1)S(1)} %pad_maximum_fusion.9), channel_id=1, source_target_pairs={{0,2},{1,3},{2,0},{3,1},{4,6},{5,7},{6,4},{7,5},{8,10},{9,11},{10,... | collective-permute-start | bytes 3145736 | tf_op jit(solution)/shard_map/ppermute | solution.py:26
  251.5 18.9 %collective-permute-start.30 = (bf16[1024,512]{1,0:T(8,128)(2,1)}, bf16[1024,512]{1,0:T(8,128)(2,1)}, u32[]{:S(2)}, u32[]{:S(2)}) collective-permute-start(bf16[1024,512]{1,0:T(8,128)(2,1)} %pad_maximum_fusion.10), channel_id=1, source_target_pairs={{0,4},{1,5},{2,6},{3,7},{4,0},{5,1},{6,2},{7,3},{8,12},{9,13},{10,... | collective-permute-start | bytes 3145736 | tf_op jit(solution)/shard_map/ppermute | solution.py:22
  285.6 18.4 %collective-permute-start.31 = (bf16[528,384]{1,0:T(8,128)(2,1)S(1)}, bf16[528,384]{1,0:T(8,128)(2,1)S(1)}, u32[]{:S(2)}, u32[]{:S(2)}) collective-permute-start(bf16[528,384]{1,0:T(8,128)(2,1)S(1)} %get-tuple-element.56), channel_id=1, source_target_pairs={{0,48},{8,56},{16,0},{24,8},{32,16},{40,24},{48,32},{56,40},{64,11... | collective-permute-start | bytes 1216520 | tf_op jit(solution)/shard_map/ppermute | solution.py:249
  292.8 13.4 %collective-permute-start.32 = (bf16[528,384]{1,0:T(8,128)(2,1)S(1)}, bf16[528,384]{1,0:T(8,128)(2,1)S(1)}, u32[]{:S(2)}, u32[]{:S(2)}) collective-permute-start(bf16[528,384]{1,0:T(8,128)(2,1)S(1)} %get-tuple-element.57), channel_id=1, source_target_pairs={{0,32},{8,40},{16,48},{24,56},{32,0},{40,8},{48,16},{56,24},{64,96... | collective-permute-start | bytes 1216520 | tf_op jit(solution)/shard_map/ppermute | solution.py:249
  310.6 16.7 %collective-permute-start.34 = (bf16[4,528,256]{2,1,0:T(8,128)(2,1)S(1)}, bf16[4,528,256]{2,1,0:T(8,128)(2,1)S(1)}, u32[]{:S(2)}, u32[]{:S(2)}) collective-permute-start(bf16[4,528,256]{2,1,0:T(8,128)(2,1)S(1)} %pad_maximum_fusion.6), channel_id=1, source_target_pairs={{0,64},{8,72},{16,80},{24,88},{32,96},{40,104},{48,112},{56,120},{... | collective-permute-start | bytes 3244040 | tf_op jit(solution)/shard_map/ppermute | solution.py:255
  392.7 27.8 %collective-permute-start.39 = (bf16[1024,512]{1,0:T(8,128)(2,1)}, bf16[1024,512]{1,0:T(8,128)(2,1)}, u32[]{:S(2)}, u32[]{:S(2)}) collective-permute-start(bf16[1024,512]{1,0:T(8,128)(2,1)} %pad_maximum_fusion.11), channel_id=1, source_target_pairs={{0,2},{1,3},{2,0},{3,1},{4,6},{5,7},{6,4},{7,5},{8,10},{9,11},{10,... | collective-permute-start | bytes 3145736 | tf_op jit(solution)/shard_map/ppermute | solution.py:26
  397.9 26.7 %collective-permute-start.41 = (bf16[1024,512]{1,0:T(8,128)(2,1)}, bf16[1024,512]{1,0:T(8,128)(2,1)S(1)}, u32[]{:S(2)}, u32[]{:S(2)}) collective-permute-start(bf16[1024,512]{1,0:T(8,128)(2,1)} %pad_maximum_fusion.12), channel_id=1, source_target_pairs={{0,4},{1,5},{2,6},{3,7},{4,0},{5,1},{6,2},{7,3},{8,12},{9,13},{10,... | collective-permute-start | bytes 3145736 | tf_op jit(solution)/shard_map/ppermute | solution.py:22
  423.0 14.2 %collective-permute-start.40 = (bf16[512,512]{1,0:T(8,128)(2,1)}, bf16[512,512]{1,0:T(8,128)(2,1)}, u32[]{:S(2)}, u32[]{:S(2)}) collective-permute-start(bf16[512,512]{1,0:T(8,128)(2,1)} %fusion.35), channel_id=1, source_target_pairs={{0,4},{1,5},{2,6},{3,7},{4,0},{5,1},{6,2},{7,3},{8,12},{9,13},{10,... | collective-permute-start | bytes 1572872 | tf_op jit(solution)/shard_map/ppermute | solution.py:22
  427.0 15.2 %collective-permute-start.42 = (bf16[512,512]{1,0:T(8,128)(2,1)}, bf16[512,512]{1,0:T(8,128)(2,1)}, u32[]{:S(2)}, u32[]{:S(2)}) collective-permute-start(bf16[512,512]{1,0:T(8,128)(2,1)} %fusion.34), channel_id=1, source_target_pairs={{0,1},{1,2},{2,3},{3,0},{4,5},{5,6},{6,7},{7,4},{8,9},{9,10},{10,1... | collective-permute-start | bytes 1572872 | tf_op jit(solution)/shard_map/ppermute | solution.py:26
  429.2 15.3 %collective-permute-start.43 = (bf16[512,512]{1,0:T(8,128)(2,1)}, bf16[512,512]{1,0:T(8,128)(2,1)}, u32[]{:S(2)}, u32[]{:S(2)}) collective-permute-start(bf16[512,512]{1,0:T(8,128)(2,1)} %fusion.33), channel_id=1, source_target_pairs={{0,3},{1,0},{2,1},{3,2},{4,7},{5,4},{6,5},{7,6},{8,11},{9,8},{10,9... | collective-permute-start | bytes 1572872 | tf_op jit(solution)/shard_map/ppermute | solution.py:26
  (34 other events, 408.2 us)

commit v2 on v1

v2 whole, which is shorter than its diff:
```python
import jax
import jax.numpy as jnp
from jax import lax
from jax.experimental import pallas as pl
from jax.experimental.pallas import tpu as pltpu
from jax.sharding import PartitionSpec as P

D1 = 1536
H1 = 24
D2 = 4096
H2 = 32
WIN = 512
EXT = 16
BF16 = jnp.bfloat16
F32 = jnp.float32
MASKED = -1e30
SCORE_FACTOR = 128 ** (-0.5) * 1.4426950408889634

PLACES = ((0, 0), (1, 0), (0, 1), (0, 3), (0, 2), (1, 2), (1, 1), (1, 3))


def flip_x(value):
    return lax.ppermute(value, "blk", [(i, i ^ 4) for i in range(8)])


def turn_z(value, steps):
    return lax.ppermute(value, "blk", [(i, (i & 4) | ((i + steps) & 3)) for i in range(8)])


def gather_blk(own):
    across = flip_x(own)
    behind = turn_z(own, 1)
    ahead = turn_z(own, 3)
    first = jnp.concatenate([own, across], axis=0)
    second = jnp.concatenate([ahead, behind], axis=0)
    opposite = turn_z(first, 2)
    diagonal = flip_x(second)
    near = jnp.concatenate([first, second], axis=0)
    far = jnp.concatenate([opposite, diagonal], axis=0)
    return near, far


def reduce_blk(near, far):
    count = near.shape[0] // 4
    opposite = turn_z(far[: 2 * count], 2)
    diagonal = flip_x(far[2 * count :])

    def plus(block, other):
        return near[block * count : (block + 1) * count].astype(F32) + other.astype(F32)

    across = flip_x(plus(1, opposite[count:]).astype(BF16))
    behind = turn_z(plus(2, diagonal[:count]).astype(BF16), 1)
    ahead = turn_z(plus(3, diagonal[count:]).astype(BF16), 3)
    return (
        plus(0, opposite[:count])
        + across.astype(F32)
        + behind.astype(F32)
        + ahead.astype(F32)
    )


def normalize(values):
    floats = values.astype(F32)
    return floats * lax.rsqrt(jnp.mean(floats * floats, axis=-1, keepdims=True) + 1e-06)


def dot(left, right):
    return jnp.dot(left, right, preferred_element_type=F32)


def dot_t(left, right):
    return lax.dot_general(left, right, (((1,), (1,)), ((), ())), preferred_element_type=F32)


def window_kernel(info, qkv, halo, out):
    rows, width, size, stride = 128, D1 // 8, D1 // H1, 128 + EXT
    key_count = WIN + rows
    i = lax.broadcasted_iota(jnp.int32, (rows, key_count), 0)
    j = lax.broadcasted_iota(jnp.int32, (rows, key_count), 1)
    band = (j > i) & (j <= i + WIN)
    seq_position = info[8]
    for n in range(8):
        place = info[n]
        keys, values = [], []
        for k in range(n - 4, n + 1):
            if k >= 0:
                start = pl.multiple_of(info[k] * stride, 16)
                block = qkv[pl.ds(start, rows), :]
                keys.append(block[:, width : 2 * width])
                values.append(block[:, 2 * width :])
            else:
                block = halo[(k + 4) * rows : (k + 5) * rows, :]
                keys.append(block[:, :width])
                values.append(block[:, width:])
        keys = jnp.concatenate(keys, axis=0)
        values = jnp.concatenate(values, axis=0)
        queries = qkv[pl.ds(pl.multiple_of(place * stride, 16), rows), :width]
        allowed = band
        if n < 4:
            allowed = band & (j + ((n - 4) * rows + seq_position * 1024) >= 0)
        parts = []
        for h in range(width // size):
            cut = slice(h * size, (h + 1) * size)
            scores = lax.dot_general(
                queries[:, cut], keys[:, cut], (((1,), (1,)), ((), ())),
                preferred_element_type=F32,
            ) * size ** (-0.5)
            scores = jnp.where(allowed, scores, MASKED)
            largest = jnp.max(scores, axis=-1, keepdims=True)
            weights = jnp.exp(scores - largest)
            total = jnp.sum(weights, axis=-1, keepdims=True)
            parts.append(dot(weights.astype(BF16), values[:, cut]) / total)
        out[pl.ds(pl.multiple_of(place * rows, 16), rows), :] = jnp.concatenate(
            parts, axis=1
        ).astype(BF16)


def window_attend(info, qkv, halo):
    vmem = pl.BlockSpec(memory_space=pltpu.VMEM)
    return pl.pallas_call(
        window_kernel,
        out_shape=jax.ShapeDtypeStruct((1024, D1 // 8), BF16),
        in_specs=[pl.BlockSpec(memory_space=pltpu.SMEM), vmem, vmem],
        out_specs=vmem,
        compiler_params=pltpu.CompilerParams(vmem_limit_bytes=40 * 2**20),
        cost_estimate=pl.CostEstimate(
            flops=24 * 128 * 640 * 256, bytes_accessed=2 * 2**20, transcendentals=24 * 128 * 640
        ),
        name="window_attend",
    )(info, qkv, halo)


def project_kernel(info, pooled, widen, weights, valid, chunks, wide_own, total, squares):
    step = pl.program_id(0)
    me, y = info[8], info[9]

    @pl.when(step == 0)
    def _():
        total[...] = jnp.zeros_like(total)
        squares[...] = jnp.zeros_like(squares)

    wide = dot(pooled[...], widen[...]).astype(BF16)
    floats = wide.astype(F32)
    squares[...] += jnp.broadcast_to(
        jnp.sum(floats * floats, axis=-1, keepdims=True), squares.shape
    )
    for i in range(3):
        total[:, i * 512 : (i + 1) * 512] += dot(wide, weights[i])

    @pl.when(step == me)
    def _():
        for p in range(8):
            start = pl.multiple_of(info[p] * 64, 64)
            wide_own[pl.ds(start, 64), :] = wide[p * 64 : (p + 1) * 64]

    @pl.when(step == 7)
    def _():
        scale = lax.rsqrt(squares[...] / D2 + 1e-06)
        for k in range(4):
            head = (y + k) & 3
            for i in range(3):
                cut = slice(i * 128, (i + 1) * 128)
                lanes = pl.ds(pl.multiple_of(i * 512 + head * 128, 128), 128)
                part = total[:, lanes] * (scale * SCORE_FACTOR if i == 0 else scale)
                part = part.astype(BF16)
                for p in range(8):
                    start = pl.multiple_of(info[p] * 64, 64)
                    chunks[k, pl.ds(start, 64), cut] = part[p * 64 : (p + 1) * 64]
                chunks[k, 512:, cut] = valid[...]


def project_two(info, pooled, widen, weights, valid):
    return pl.pallas_call(
        project_kernel,
        out_shape=(
            jax.ShapeDtypeStruct((4, 512 + EXT, 384), BF16),
            jax.ShapeDtypeStruct((512, 512), BF16),
        ),
        grid_spec=pltpu.PrefetchScalarGridSpec(
            num_scalar_prefetch=1,
            grid=(8,),
            in_specs=[
                pl.BlockSpec((512, D1), lambda s, info: (0, 0)),
                pl.BlockSpec((D1, 512), lambda s, info: (0, s)),
                pl.BlockSpec((3, 512, 512), lambda s, info: (0, s, 0)),
                pl.BlockSpec((EXT, 128), lambda s, info: (0, 0)),
            ],
            out_specs=(
                pl.BlockSpec((4, 512 + EXT, 384), lambda s, info: (0, 0, 0)),
                pl.BlockSpec((512, 512), lambda s, info: (0, 0)),
            ),
            scratch_shapes=[pltpu.VMEM((512, 1536), F32), pltpu.VMEM((512, 128), F32)],
        ),
        compiler_params=pltpu.CompilerParams(vmem_limit_bytes=40 * 2**20),
        cost_estimate=pl.CostEstimate(
            flops=4 * 512 * 4096 * 1536, bytes_accessed=28 * 2**20, transcendentals=512
        ),
        name="project_two",
    )(info, pooled, widen, weights, valid)


def causal_kernel(own_part, info, queries, kv, start, start_stats, out, out_stats, keys, values, even, odd):
    half, core, y = info[0], info[1], info[2]
    slot = pl.program_id(0)
    own_pair = (y + slot) & 3

    @pl.when(slot == 0)
    def _():
        def prepare(block, _):
            count = jnp.sum(kv[block, 512 : 512 + EXT, :128].astype(F32))
            row = lax.broadcasted_iota(jnp.int32, (512, 128), 0).astype(F32)
            lane = lax.broadcasted_iota(jnp.int32, (512, 128), 1)
            keys[block, :, :128] = kv[block, :512, :128]
            keys[block, :, 128:] = jnp.where((lane == 0) & (row >= count), MASKED, 0.0).astype(BF16)
            values[block] = kv[block, :512, 128:].T
            return 0

        lax.fori_loop(0, 8, prepare, 0)

    lane = lax.broadcasted_iota(jnp.int32, (512, 128), 1)
    query = jnp.concatenate([queries[0], jnp.where(lane == 0, 1.0, 0.0).astype(BF16)], axis=1)

    def block_of(pair, which):
        return (which ^ core) * 4 + ((pair - y) & 3)

    def scores_of(pair, which):
        return lax.dot_general(
            keys[block_of(pair, which)], query, (((1,), (1,)), ((), ())), preferred_element_type=F32
        )

    def absorb(scores, pair, which, carry, edge):
        largest, total, sums = carry
        if edge:
            key = lax.broadcasted_iota(jnp.int32, scores.shape, 0) + which * 512
            own = lax.broadcasted_iota(jnp.int32, scores.shape, 1) + core * 512
            scores = jnp.where(key <= own, scores, MASKED)
        new_largest = jnp.maximum(largest, jnp.max(scores, axis=0, keepdims=True))
        decay = jnp.exp2(largest - new_largest)
        weights = jnp.exp2(scores - new_largest)
        total = total * decay + jnp.sum(weights, axis=0, keepdims=True)
        sums = sums * decay + dot(values[block_of(pair, which)], weights.astype(BF16))
        return new_largest, total, sums

    even[...] = scores_of(0, 0)

    def both(pair, carry, edge=False):
        odd[...] = scores_of(pair, 1)
        carry = absorb(even[...], pair, 0, carry, edge)
        if not edge:
            even[...] = scores_of((pair + 1) & 3, 0)
        return absorb(odd[...], pair, 1, carry, edge)

    if own_part:
        carry = (
            jnp.full((1, 512), MASKED, F32), jnp.zeros((1, 512), F32), jnp.zeros((128, 512), F32)
        )
        carry = lax.fori_loop(0, own_pair, both, carry)
        largest, total, sums = both(own_pair, carry, True)
        out[0] = sums
        out_stats[0] = jnp.concatenate([largest, total, jnp.zeros((6, 512), F32)], axis=0)
    else:
        carry = (start_stats[0, 0:1], start_stats[0, 1:2], start[0])
        _, total, sums = lax.fori_loop(0, half * 4, both, carry)
        out[0] = (sums / total).T.astype(BF16)


def causal_attend(own_part, info, queries, kv, start=None):
    def by_slot(*shape):
        return pl.BlockSpec((1, *shape), lambda s, info: (s, 0, 0))

    sums_shape = jax.ShapeDtypeStruct((4, 128, 512), F32)
    stats_shape = jax.ShapeDtypeStruct((4, 8, 512), F32)
    in_specs = [by_slot(512, 128), pl.BlockSpec((8, 512 + EXT, 256), lambda s, info: (0, 0, 0))]
    operands = [queries, kv]
    if own_part:
        def kernel(info, queries, kv, out, out_stats, *scratch):
            causal_kernel(True, info, queries, kv, None, None, out, out_stats, *scratch)

        out_shape = (sums_shape, stats_shape)
        out_specs = (by_slot(128, 512), by_slot(8, 512))
        tiles = 18
    else:
        def kernel(info, queries, kv, start, start_stats, out, *scratch):
            causal_kernel(False, info, queries, kv, start, start_stats, out, None, *scratch)

        out_shape = jax.ShapeDtypeStruct((4, 512, 128), BF16)
        out_specs = by_slot(512, 128)
        in_specs += [by_slot(128, 512), by_slot(8, 512)]
        operands += list(start)
        tiles = 32
    return pl.pallas_call(
        kernel,
        out_shape=out_shape,
        grid_spec=pltpu.PrefetchScalarGridSpec(
            num_scalar_prefetch=1,
            grid=(4,),
            in_specs=in_specs,
            out_specs=out_specs,
            scratch_shapes=[
                pltpu.VMEM((8, 512, 256), BF16),
                pltpu.VMEM((8, 128, 512), BF16),
                pltpu.VMEM((512, 512), F32),
                pltpu.VMEM((512, 512), F32),
            ],
        ),
        compiler_params=pltpu.CompilerParams(vmem_limit_bytes=40 * 2**20),
        cost_estimate=pl.CostEstimate(
            flops=tiles * 512 * 512 * 512, bytes_accessed=4 * 2**20, transcendentals=tiles * 2**18
        ),
        name="causal_own" if own_part else "causal_first_half",
    )(info, *operands)


def turn_y(value, steps):
    return lax.ppermute(
        value, "seq", [(i, (i & 9) | ((i + 2 * steps) & 6)) for i in range(16)]
    )


def flip_seq(value, bit):
    return lax.ppermute(value, "seq", [(i, i ^ bit) for i in range(16)])


def per_device(
    tokens, boundary, heads_in, heads_out, gate_up, down_weight, widen, heads_in_two, heads_out_two
):
    seq_position = lax.axis_index("seq")
    me = lax.axis_index("blk")
    rows = tokens.shape[0]
    capacity = 512
    width = D1 // 8
    block_of = jnp.stack([((me ^ (4 * x)) & 4) | ((me + z) & 3) for x, z in PLACES])
    numbers = jnp.arange(8, dtype=jnp.int32)
    place_of = jnp.sum(
        jnp.where(block_of[None, :] == numbers[:, None], numbers[None, :], 0), axis=1
    )

    heads_in_flat = heads_in.transpose(1, 2, 0).reshape(3 * width, D1)
    gate_flat, up_flat = lax.optimization_barrier((gate_up[:, 0, :], gate_up[:, 1, :]))
    share = D1 // 16
    widen_rows = lax.dynamic_slice(widen, (seq_position * share, 0), (share, 512))
    widen_rows = lax.all_gather(widen_rows, "blk", axis=1, tiled=True)
    widen_whole = lax.all_gather(widen_rows, "seq", axis=0, tiled=True)

    normed = normalize(tokens).astype(BF16)
    marks_row = jnp.pad(boundary.astype(BF16)[None, :], ((0, EXT - 1), (0, D1 - rows)))
    near, far = gather_blk(jnp.concatenate([normed, marks_row], axis=0))
    marks = jnp.concatenate([near, far], axis=0).reshape(8, rows + EXT, D1)[:, rows, :rows]
    qkv = jnp.concatenate(
        [dot_t(near, heads_in_flat).astype(BF16), dot_t(far, heads_in_flat).astype(BF16)], axis=0
    )
    edge = jnp.concatenate(
        [
            lax.dynamic_slice(qkv, (place_of[n] * (rows + EXT), width), (rows, 2 * width))
            for n in range(4, 8)
        ],
        axis=0,
    )
    halo = lax.ppermute(edge, "seq", [(i, i + 1) for i in range(15)])
    info = jnp.concatenate([place_of, seq_position[None]]).astype(jnp.int32)
    attended = window_attend(info, qkv, halo)
    attn_near = dot(attended[: 4 * rows], heads_out).astype(BF16)
    attn_far = dot(attended[4 * rows :], heads_out).astype(BF16)
    mid_stream = (tokens.astype(F32) + reduce_blk(attn_near, attn_far)).astype(BF16)

    normed_mid = normalize(mid_stream).astype(BF16)

    def mlp(block):
        hidden = jax.nn.silu(dot(block, gate_flat)) * dot(block, up_flat)
        return dot(hidden.astype(BF16), down_weight).astype(BF16)

    near, far = gather_blk(normed_mid)
    mlp_near, mlp_far = mlp(near), mlp(far)
    marks = marks.astype(F32)
    counts = jnp.sum(marks, axis=1)
    before = jnp.sum(
        jnp.where(block_of[None, :] < block_of[:, None], counts[None, :], 0.0), axis=1
    )
    steps = jnp.arange(rows)
    running = dot(marks.astype(BF16), (steps[:, None] <= steps[None, :]).astype(BF16))
    slots = jnp.where(marks > 0.5, before[:, None] + running - 1.0, -1.0).astype(jnp.int32)
    span_count = jnp.sum(counts).astype(jnp.int32)
    targets = (block_of[:, None] * 64 + jnp.arange(64)[None, :]).reshape(capacity, 1)
    selector = (slots.reshape(1, 8 * rows) == targets).astype(BF16)
    placed = (
        dot(selector[:, : 4 * rows], mlp_near)
        + dot(selector[:, 4 * rows :], mlp_far)
        + dot(selector[:, :rows], mid_stream)
    ).astype(BF16)
    pooled_own = reduce_blk(placed[:256], placed[256:]).astype(BF16)
    pooled = jnp.concatenate(gather_blk(pooled_own), axis=0)

    level_one = (mid_stream.astype(F32) + reduce_blk(mlp_near, mlp_far)).astype(BF16)

    validity = (jnp.arange(capacity, dtype=jnp.int32) < span_count).astype(F32)
    valid_rows = jnp.pad(
        validity.reshape(4, 128).astype(BF16), ((0, EXT - 4), (0, 0))
    )
    core, y, half = seq_position & 1, (seq_position >> 1) & 3, seq_position >> 3
    info_one = jnp.concatenate([block_of, me[None], y[None]]).astype(jnp.int32)
    chunks, wide_cols = project_two(
        info_one, pooled, widen_whole, heads_in_two.transpose(1, 0, 2), valid_rows
    )
    from_behind = turn_y(chunks[1], 1)
    from_ahead = turn_y(chunks[3], 3)
    from_opposite = turn_y(chunks[2], 2)
    mine = jnp.stack([chunks[0], from_ahead, from_opposite, from_behind])
    queries, own_kv = mine[:, :capacity, :128], mine[:, :, 128:]
    first_kv = lax.ppermute(own_kv, "seq", [(i, i + 8) for i in range(8)])
    own_pair = jnp.concatenate([own_kv, flip_seq(own_kv, 1)], axis=0)
    first_pair = jnp.concatenate([first_kv, flip_seq(first_kv, 1)], axis=0)
    info_two = jnp.stack([half, core, y]).astype(jnp.int32)
    running = causal_attend(True, info_two, queries, own_pair)
    mixed = causal_attend(False, info_two, queries, first_pair, running)
    back = [mixed[0], turn_y(mixed[3], 3), turn_y(mixed[2], 2), turn_y(mixed[1], 1)]
    heads = jnp.concatenate([back[0], back[1], back[2], back[3]] * 2, axis=1)
    attended_two = lax.dynamic_slice(heads, (0, ((4 - y) & 3) * 128), (capacity, 512))

    def columns(place):
        part = lax.dynamic_slice(heads_out_two, (0, block_of[place] * 512), (512, 512))
        return dot(attended_two, part).astype(BF16)

    out_far = jnp.concatenate([columns(place) for place in range(4, 8)], axis=0)
    out_near = jnp.concatenate([columns(place) for place in range(4)], axis=0)
    level_two = (
        (wide_cols.astype(F32) + reduce_blk(out_near, out_far)) * validity[:, None]
    ).astype(BF16)
    return (level_one, level_two)


def solution(mesh):
    placed = (
        P(("seq", "blk"), None),
        P(("seq", "blk")),
        P(None, None, "blk"),
        P("blk", None),
        P(None, None, "blk"),
        P("blk", None),
        P(None, "blk"),
        P(None, None, "blk"),
        P("blk", None),
    )
    return jax.shard_map(
        per_device,
        mesh=mesh,
        in_specs=placed,
        out_specs=(P(("seq", "blk"), None), P("seq", "blk")),
        check_vma=False,
    )
```

time: 455 us -> 433 us (0.952)
  blocking collectives: 0 us -> 32.2 us
  local copies, waits for them, and re-layouts: 51.6 us -> 24.4 us
  starting transfers between devices: 75.2 us -> 48.3 us
  between operations: 4.5 us -> 18.3 us
  Pallas kernels: 63.5 us -> 55.2 us
    ppermute x21, waiting for transfers between devices: 96.8 us -> 64.5 us  [turn_z(): lax.ppermute(value, 'blk', [(i, i & 4 | i + steps & 3) for i in range(8)])]
    all_gather x0 -> x1, blocking collectives: none -> 32.2 us  [per_device(): widen_rows = lax.all_gather(widen_rows, 'blk', axis=1, tiled=True)]
    ppermute x0 -> x1, waiting for transfers between devices: none -> 26.7 us  [per_device(): first_kv = lax.ppermute(own_kv, 'seq', [(i, i + 8) for i in range(8)])]
    ppermute x2, waiting for transfers between devices: 19.7 us -> 0.01 us  [flip_seq(): return lax.ppermute(value, 'seq', [(i, i ^ bit) for i in range(16)])]
    optimization_barrier x1 -> x0, local copies, waits for them, and re-layouts: 16.7 us -> none  [per_device(): lax.optimization_barrier((heads_in.reshape(D1, 3 * width), gate_up[:, 0,...]
    ppermute x14, waiting for transfers between devices: 48.3 us -> 64.7 us  [flip_x(): return lax.ppermute(value, 'blk', [(i, i ^ 4) for i in range(8)])]
    unnamed x59 -> x80, local copies, waits for them, and re-layouts: 23.8 us -> 9.72 us
    ppermute x21, starting transfers between devices: 35 us -> 21.7 us  [turn_z(): lax.ppermute(value, 'blk', [(i, i & 4 | i + steps & 3) for i in range(8)])]
  transfers between devices with their start and end apart: 44 -> 46, of which waited for: 32 -> 30; matrix products, arithmetic and copies ran while one was open for 15% -> 18% of each run, Pallas kernels for 0% -> 9%
where the time goes in v2:
time: 433 us; the launch traced here: 427 us
  waiting for transfers between devices  191 us (44%)
  Pallas kernels  55.2 us (13%)
  starting transfers between devices  48.3 us (11%)
  matrix products  38.9 us (9%)
  blocking collectives  32.2 us (7%)
  local copies, waits for them, and re-layouts  24.4 us (6%)
  other arithmetic  18.4 us (4%)
  between operations  18.3 us (4%)
    ppermute x14, waiting for transfers between devices, flip_x(): return lax.ppermute(value, 'blk', [(i, i ^ 4) for i in range(8)])  64.7 us
    ppermute x21, waiting for transfers between devices, turn_z(): lax.ppermute(value, 'blk', [(i, i & 4 | i + steps & 3) for i in range(8)])  64.5 us
    dot_general x18, matrix products, dot(): return jnp.dot(left, right, preferred_element_type=F32)  34.3 us
    all_gather x1, blocking collectives, per_device(): widen_rows = lax.all_gather(widen_rows, 'blk', axis=1, tiled=True)  32.2 us
    pallas_call x2, Pallas kernels, causal_attend(): pl.pallas_call(kernel, out_shape=out_shape, grid_spec=pltpu.PrefetchScala...  28.2 us
    ppermute x1, waiting for transfers between devices, per_device(): first_kv = lax.ppermute(own_kv, 'seq', [(i, i + 8) for i in range(8)])  26.7 us
    ppermute x21, starting transfers between devices, turn_z(): lax.ppermute(value, 'blk', [(i, i & 4 | i + steps & 3) for i in range(8)])  21.7 us
    ppermute x1, waiting for transfers between devices, per_device(): halo = lax.ppermute(edge, 'seq', [(i, i + 1) for i in range(15)])  18.6 us
  transfers between devices with their start and end apart: 46, of which 30 were waited for; matrix products, arithmetic and copies ran while one was open for 18% of the time, Pallas kernels for 9%

profile of v2, /device:TPU:6, one launch (start us, length us, event | category | flops | bytes accessed | tf_op | source)
XLA Modules:
  0.0 426.5 jit_solution(7267892154798886038)
XLA Ops:
  8.3 32.2 %all_gather.6 = bf16[96,4096]{1,0:T(8,128)(2,1)} all-gather(bf16[96,512]{1,0:T(8,128)(2,1)S(1)} %constant_dynamic-slice_fusion), channel_id=1, replica_groups=mesh['seq'=16,'blk'=8] {'blk'}, dimensions={1}, use_global_device_ids=true | all-gather | bytes 884736 | tf_op jit(solution)/shard_map/all_gather | solution.py:342
  48.3 5.9 %fusion.81 = (bf16[1536,1,512]{2,1,0:T(2,128)(2,1)}, bf16[1536,1,512]{2,1,0:T(2,128)(2,1)}) fusion(bf16[1536,2,512]{2,1,0:T(2,128)(2,1)S(1)} %copy-done.2), kind=kLoop, calls=%fused_computation.192 | loop fusion | bytes 6291456 | tf_op jit(solution)/shard_map/slice | solution.py:339
  65.7 3.0 convolution_convert_fusion.4
  68.7 14.5 %collective-permute-done.4 = bf16[288,1536]{1,0:T(8,128)(2,1)S(1)} collective-permute-done((bf16[288,1536]{1,0:T(8,128)(2,1)S(1)}, bf16[288,1536]{1,0:T(8,128)(2,1)S(1)}, u32[]{:S(2)}, u32[]{:S(2)}) %collective-permute-start.4) | collective-permute-done | bytes 884768 | tf_op jit(solution)/shard_map/ppermute | solution.py:23
  88.2 18.6 %collective-permute-done.5.halo = bf16[512,384]{1,0:T(8,128)(2,1)S(1)} collective-permute-done((bf16[512,384]{1,0:T(8,128)(2,1)S(1)}, bf16[512,384]{1,0:T(8,128)(2,1)S(1)}, u32[]{:S(2)}, u32[]{:S(2)}) %collective-permute-start.5) | collective-permute-done | bytes 393248 | tf_op jit(solution)/shard_map/ppermute | solution.py:359
  106.8 8.9 %window_attend.1 = bf16[1024,192]{1,0:T(8,128)(2,1)S(1)} custom-call(s32[9]{0:T(128)S(1)} %pad_add_fusion.info, bf16[1152,576]{1,0:T(8,128)(2,1)S(1)} %pad_maximum_fusion.qkv, bf16[512,384]{1,0:T(8,128)(2,1)S(1)} %collective-permute-done.5.halo), custom_call_target="tpu_custom_call" | custom-call | flops 503316480 | bytes 2097152 | tf_op jit(solution)/shard_map/window_attend/pallas_call | solution.py:120
  123.0 17.8 %collective-permute-done.8 = bf16[256,1536]{1,0:T(8,128)(2,1)S(1)} collective-permute-done((bf16[256,1536]{1,0:T(8,128)(2,1)}, bf16[256,1536]{1,0:T(8,128)(2,1)S(1)}, u32[]{:S(2)}, u32[]{:S(2)}) %collective-permute-start.8) | collective-permute-done | bytes 786464 | tf_op jit(solution)/shard_map/ppermute | solution.py:23
  146.7 5.0 %collective-permute-done.10 = bf16[128,1536]{1,0:T(8,128)(2,1)S(1)} collective-permute-done((bf16[128,1536]{1,0:T(8,128)(2,1)S(1)}, bf16[128,1536]{1,0:T(8,128)(2,1)S(1)}, u32[]{:S(2)}, u32[]{:S(2)}) %collective-permute-start.10) | collective-permute-done | bytes 393248 | tf_op jit(solution)/shard_map/ppermute | solution.py:27
  151.7 3.4 collective-permute-done.9
  157.2 3.4 collective-permute-start.12
  165.2 18.2 %collective-permute-done.13 = bf16[128,1536]{1,0:T(8,128)(2,1)S(1)} collective-permute-done((bf16[128,1536]{1,0:T(8,128)(2,1)S(1)}, bf16[128,1536]{1,0:T(8,128)(2,1)S(1)}, u32[]{:S(2)}, u32[]{:S(2)}) %collective-permute-start.13) | collective-permute-done | bytes 393248 | tf_op jit(solution)/shard_map/ppermute | solution.py:27
  187.2 5.2 %convolution_convert_fusion.1 = bf16[512,1536]{1,0:T(8,128)(2,1)} fusion(bf16[512,1536]{1,0:T(8,128)(2,1)} %param.14, f32[512,512]{1,0:T(8,128)} %fusion.45, bf16[1536,512]{1,0:T(8,128)(2,1)S(1)} %copy-done.16, bf16[128,1536]{1,0:T(8,128)(2,1)} %copy-done.27, bf16[128,1536]{1,0:T(8,128)(2,1)} %copy-done.28, bf16[128,1536]{1,0:T(8,128)(2,1)} %copy-done.26, ...), kind=kOutput, calls=%fused_computation.3 | convolution fusion | flops 1619263488 | bytes 7340032 | tf_op jit(solution)/shard_map/dot_general | solution.py:68
  192.4 4.1 fusion.27
  202.0 4.5 %convolution_convert_fusion = bf16[512,1536]{1,0:T(8,128)(2,1)S(1)} fusion(bf16[512,1536]{1,0:T(8,128)(2,1)} %param.14, f32[512,512]{1,0:T(8,128)} %fusion.89, bf16[512,1536]{1,0:T(8,128)(2,1)} %copy-done.25, bf16[1536,512]{1,0:T(8,128)(2,1)} %get-tuple-element.9), kind=kOutput, calls=%fused_computation.2 | convolution fusion | flops 1612972032 | bytes 7340032 | tf_op jit(solution)/shard_map/dot_general | solution.py:68
  206.6 3.4 convolution_add_fusion.1
  211.9 7.7 %collective-permute-done.23 = bf16[128,1536]{1,0:T(8,128)(2,1)S(1)} collective-permute-done((bf16[128,1536]{1,0:T(8,128)(2,1)S(1)}, bf16[128,1536]{1,0:T(8,128)(2,1)S(1)}, u32[]{:S(2)}, u32[]{:S(2)}) %collective-permute-start.23) | collective-permute-done | bytes 393248 | tf_op jit(solution)/shard_map/ppermute | solution.py:23
  219.6 5.7 %collective-permute-done.21 = bf16[128,1536]{1,0:T(8,128)(2,1)S(1)} collective-permute-done((bf16[128,1536]{1,0:T(8,128)(2,1)S(1)}, bf16[128,1536]{1,0:T(8,128)(2,1)S(1)}, u32[]{:S(2)}, u32[]{:S(2)}) %collective-permute-start.21) | collective-permute-done | bytes 393248 | tf_op jit(solution)/shard_map/ppermute | solution.py:27
  231.3 3.7 collective-permute-done.24
  247.8 3.4 collective-permute-done.29
  254.1 18.1 %project_two.1 = (bf16[4,528,384]{2,1,0:T(8,128)(2,1)S(1)}, bf16[512,512]{1,0:T(8,128)(2,1)S(1)}) custom-call(s32[10]{0:T(128)S(1)} %concatenate.89.info, bf16[512,1536]{1,0:T(8,128)(2,1)S(1)} %constant_dynamic-update-slice_fusion.14.pooled, bf16[1536,4096]{1,0:T(8,128)(2,1)} %all-gather.2.cloned.1.call-done.widen, bf16[3,4096,512]{2,1,0:T(8,128)(2,1)} %bitcast.86, ...), custom_call_target="tpu_custom_call" | custom-call | flops 12884901888 | bytes 29360128 | tf_op jit(solution)/shard_map/project_two/pallas_call | solution.py:173
  272.4 3.6 collective-permute-start.33
  281.6 6.1 %collective-permute-done.32 = bf16[528,384]{1,0:T(8,128)(2,1)S(1)} collective-permute-done((bf16[528,384]{1,0:T(8,128)(2,1)S(1)}, bf16[528,384]{1,0:T(8,128)(2,1)S(1)}, u32[]{:S(2)}, u32[]{:S(2)}) %collective-permute-start.32) | collective-permute-done | bytes 405536 | tf_op jit(solution)/shard_map/ppermute | solution.py:315
  291.0 26.7 %collective-permute-done.34 = bf16[4,528,256]{2,1,0:T(8,128)(2,1)} collective-permute-done((bf16[4,528,256]{2,1,0:T(8,128)(2,1)}, bf16[4,528,256]{2,1,0:T(8,128)(2,1)}, u32[]{:S(2)}, u32[]{:S(2)}) %collective-permute-start.34) | collective-permute-done | bytes 1081376 | tf_op jit(solution)/shard_map/ppermute | solution.py:409
  321.1 11.4 %causal_own.1 = (f32[4,128,512]{2,1,0:T(8,128)S(1)}, f32[4,8,512]{2,1,0:T(8,128)S(1)}) custom-call(s32[3]{0:T(128)S(1)} %pad_add_fusion.1.info, bf16[4,512,128]{2,1,0:T(8,128)(2,1)S(1)} %pad_maximum_fusion.13.queries, bf16[8,528,256]{2,1,0:T(8,128)(2,1)S(1)} %pad_maximum_fusion.2.kv), custom_call_target="tpu_custom_call" | custom-call | flops 2415919104 | bytes 4194304 | tf_op jit(solution)/shard_map/causal_own/pallas_call | solution.py:291
  334.3 16.8 %causal_first_half.1 = bf16[4,512,128]{2,1,0:T(8,128)(2,1)S(1)} custom-call(s32[3]{0:T(128)S(1)} %pad_add_fusion.1.info, bf16[4,512,128]{2,1,0:T(8,128)(2,1)S(1)} %pad_maximum_fusion.13.queries, bf16[8,528,256]{2,1,0:T(8,128)(2,1)S(1)} %pad_maximum_fusion.1.kv, f32[4,128,512]{2,1,0:T(8,128)S(1)} %get-tuple-element.12.start, ...), custom_call_target="tpu_custom_call" | custom-call | flops 4294967296 | bytes 4194304 | tf_op jit(solution)/shard_map/causal_first_half/pallas_call | solution.py:291
  353.7 3.8 collective-permute-done.37
  371.9 3.5 collective-permute-start.40
  379.4 14.1 %collective-permute-done.42 = bf16[1024,512]{1,0:T(8,128)(2,1)} collective-permute-done((bf16[1024,512]{1,0:T(8,128)(2,1)}, bf16[1024,512]{1,0:T(8,128)(2,1)}, u32[]{:S(2)}, u32[]{:S(2)}) %collective-permute-start.42) | collective-permute-done | bytes 1048608 | tf_op jit(solution)/shard_map/ppermute | solution.py:23
  396.5 3.3 collective-permute-done.40
  400.4 4.7 %collective-permute-done.20 = bf16[128,1536]{1,0:T(8,128)(2,1)S(1)} collective-permute-done((bf16[128,1536]{1,0:T(8,128)(2,1)S(1)}, bf16[128,1536]{1,0:T(8,128)(2,1)S(1)}, u32[]{:S(2)}, u32[]{:S(2)}) %collective-permute-start.20) | collective-permute-done | bytes 393248 | tf_op jit(solution)/shard_map/ppermute | solution.py:27
  409.5 5.4 %collective-permute-done.44 = bf16[512,512]{1,0:T(8,128)(2,1)S(1)} collective-permute-done((bf16[512,512]{1,0:T(8,128)(2,1)S(1)}, bf16[512,512]{1,0:T(8,128)(2,1)S(1)}, u32[]{:S(2)}, u32[]{:S(2)}) %collective-permute-start.44) | collective-permute-done | bytes 524320 | tf_op jit(solution)/shard_map/ppermute | solution.py:27
  414.9 3.0 collective-permute-done.43
  (222 shorter events, 119.0 us)
Async XLA Ops:
  7.2 246.9 %all-gather.2.cloned.1.call-start = ((), (), s32[]{:S(2)}) async-start(), calls=%async_computation | async-start | bytes 13369344 | tf_op jit(solution)/shard_map/all_gather | solution.py:343
  43.9 13.9 %collective-permute-start.2 = (bf16[144,1536]{1,0:T(8,128)(2,1)}, bf16[144,1536]{1,0:T(8,128)(2,1)S(1)}, u32[]{:S(2)}, u32[]{:S(2)}) collective-permute-start(bf16[144,1536]{1,0:T(8,128)(2,1)} %pad_maximum_fusion.14), channel_id=1, source_target_pairs={{0,1},{1,2},{2,3},{3,0},{4,5},{5,6},{6,7},{7,4},{8,9},{9,10},{10,1... | collective-permute-start | bytes 1327112 | tf_op jit(solution)/shard_map/ppermute | solution.py:27
  45.5 12.3 %collective-permute-start.1 = (bf16[144,1536]{1,0:T(8,128)(2,1)}, bf16[144,1536]{1,0:T(8,128)(2,1)S(1)}, u32[]{:S(2)}, u32[]{:S(2)}) collective-permute-start(bf16[144,1536]{1,0:T(8,128)(2,1)} %pad_maximum_fusion.14), channel_id=1, source_target_pairs={{0,3},{1,0},{2,1},{3,2},{4,7},{5,4},{6,5},{7,6},{8,11},{9,8},{10,9... | collective-permute-start | bytes 1327112 | tf_op jit(solution)/shard_map/ppermute | solution.py:27
  47.4 13.1 %collective-permute-start = (bf16[144,1536]{1,0:T(8,128)(2,1)}, bf16[144,1536]{1,0:T(8,128)(2,1)}, u32[]{:S(2)}, u32[]{:S(2)}) collective-permute-start(bf16[144,1536]{1,0:T(8,128)(2,1)} %pad_maximum_fusion.14), channel_id=1, source_target_pairs={{0,4},{1,5},{2,6},{3,7},{4,0},{5,1},{6,2},{7,3},{8,12},{9,13},{10,... | collective-permute-start | bytes 1327112 | tf_op jit(solution)/shard_map/ppermute | solution.py:23
  57.9 25.4 %collective-permute-start.4 = (bf16[288,1536]{1,0:T(8,128)(2,1)S(1)}, bf16[288,1536]{1,0:T(8,128)(2,1)S(1)}, u32[]{:S(2)}, u32[]{:S(2)}) collective-permute-start(bf16[288,1536]{1,0:T(8,128)(2,1)S(1)} %pad_maximum_fusion.10), channel_id=1, source_target_pairs={{0,4},{1,5},{2,6},{3,7},{4,0},{5,1},{6,2},{7,3},{8,12},{9,13},{10,... | collective-permute-start | bytes 2654216 | tf_op jit(solution)/shard_map/ppermute | solution.py:23
  61.5 21.8 %collective-permute-start.3 = (bf16[288,1536]{1,0:T(8,128)(2,1)S(1)}, bf16[288,1536]{1,0:T(8,128)(2,1)S(1)}, u32[]{:S(2)}, u32[]{:S(2)}) collective-permute-start(bf16[288,1536]{1,0:T(8,128)(2,1)S(1)} %pad_maximum_fusion.9), channel_id=1, source_target_pairs={{0,2},{1,3},{2,0},{3,1},{4,6},{5,7},{6,4},{7,5},{8,10},{9,11},{10,... | collective-permute-start | bytes 2654216 | tf_op jit(solution)/shard_map/ppermute | solution.py:27
  85.9 20.9 %collective-permute-start.5 = (bf16[512,384]{1,0:T(8,128)(2,1)S(1)}, bf16[512,384]{1,0:T(8,128)(2,1)S(1)}, u32[]{:S(2)}, u32[]{:S(2)}) collective-permute-start(bf16[512,384]{1,0:T(8,128)(2,1)S(1)} %pad_maximum_fusion.15), channel_id=1, source_target_pairs={{0,8},{8,16},{16,24},{24,32},{32,40},{40,48},{48,56},{56,64},{64,7... | collective-permute-start | bytes 1179656 | tf_op jit(solution)/shard_map/ppermute | solution.py:359
  117.5 23.3 %collective-permute-start.8 = (bf16[256,1536]{1,0:T(8,128)(2,1)}, bf16[256,1536]{1,0:T(8,128)(2,1)S(1)}, u32[]{:S(2)}, u32[]{:S(2)}) collective-permute-start(bf16[256,1536]{1,0:T(8,128)(2,1)} %get-tuple-element.42), channel_id=1, source_target_pairs={{0,4},{1,5},{2,6},{3,7},{4,0},{5,1},{6,2},{7,3},{8,12},{9,13},{10,... | collective-permute-start | bytes 2359304 | tf_op jit(solution)/shard_map/ppermute | solution.py:23
  118.7 22.1 %collective-permute-start.6 = (bf16[256,1536]{1,0:T(8,128)(2,1)}, bf16[256,1536]{1,0:T(8,128)(2,1)S(1)}, u32[]{:S(2)}, u32[]{:S(2)}) collective-permute-start(bf16[256,1536]{1,0:T(8,128)(2,1)} %get-tuple-element.41), channel_id=1, source_target_pairs={{0,2},{1,3},{2,0},{3,1},{4,6},{5,7},{6,4},{7,5},{8,10},{9,11},{10,... | collective-permute-start | bytes 2359304 | tf_op jit(solution)/shard_map/ppermute | solution.py:27
  141.7 10.0 %collective-permute-start.10 = (bf16[128,1536]{1,0:T(8,128)(2,1)S(1)}, bf16[128,1536]{1,0:T(8,128)(2,1)S(1)}, u32[]{:S(2)}, u32[]{:S(2)}) collective-permute-start(bf16[128,1536]{1,0:T(8,128)(2,1)S(1)} %get-tuple-element.27), channel_id=1, source_target_pairs={{0,3},{1,0},{2,1},{3,2},{4,7},{5,4},{6,5},{7,6},{8,11},{9,8},{10,9... | collective-permute-start | bytes 1179656 | tf_op jit(solution)/shard_map/ppermute | solution.py:27
  144.6 10.4 %collective-permute-start.9 = (bf16[128,1536]{1,0:T(8,128)(2,1)S(1)}, bf16[128,1536]{1,0:T(8,128)(2,1)S(1)}, u32[]{:S(2)}, u32[]{:S(2)}) collective-permute-start(bf16[128,1536]{1,0:T(8,128)(2,1)S(1)} %get-tuple-element.26), channel_id=1, source_target_pairs={{0,1},{1,2},{2,3},{3,0},{4,5},{5,6},{6,7},{7,4},{8,9},{9,10},{10,1... | collective-permute-start | bytes 1179656 | tf_op jit(solution)/shard_map/ppermute | solution.py:27
  144.6 10.4 %collective-permute-start.7 = (bf16[128,1536]{1,0:T(8,128)(2,1)S(1)}, bf16[128,1536]{1,0:T(8,128)(2,1)S(1)}, u32[]{:S(2)}, u32[]{:S(2)}) collective-permute-start(bf16[128,1536]{1,0:T(8,128)(2,1)S(1)} %get-tuple-element.40), channel_id=1, source_target_pairs={{0,4},{1,5},{2,6},{3,7},{4,0},{5,1},{6,2},{7,3},{8,12},{9,13},{10,... | collective-permute-start | bytes 1179656 | tf_op jit(solution)/shard_map/ppermute | solution.py:23
  157.2 26.1 %collective-permute-start.13 = (bf16[128,1536]{1,0:T(8,128)(2,1)S(1)}, bf16[128,1536]{1,0:T(8,128)(2,1)S(1)}, u32[]{:S(2)}, u32[]{:S(2)}) collective-permute-start(bf16[128,1536]{1,0:T(8,128)(2,1)S(1)} %fusion.33), channel_id=1, source_target_pairs={{0,1},{1,2},{2,3},{3,0},{4,5},{5,6},{6,7},{7,4},{8,9},{9,10},{10,1... | collective-permute-start | bytes 1179656 | tf_op jit(solution)/shard_map/ppermute | solution.py:27
  157.2 26.1 %collective-permute-start.12 = (bf16[128,1536]{1,0:T(8,128)(2,1)S(1)}, bf16[128,1536]{1,0:T(8,128)(2,1)S(1)}, u32[]{:S(2)}, u32[]{:S(2)}) collective-permute-start(bf16[128,1536]{1,0:T(8,128)(2,1)S(1)} %fusion.33), channel_id=1, source_target_pairs={{0,3},{1,0},{2,1},{3,2},{4,7},{5,4},{6,5},{7,6},{8,11},{9,8},{10,9... | collective-permute-start | bytes 1179656 | tf_op jit(solution)/shard_map/ppermute | solution.py:27
  165.1 31.3 %collective-permute-start.14 = (bf16[256,1536]{1,0:T(8,128)(2,1)}, bf16[256,1536]{1,0:T(8,128)(2,1)}, u32[]{:S(2)}, u32[]{:S(2)}) collective-permute-start(bf16[256,1536]{1,0:T(8,128)(2,1)} %pad_maximum_fusion.11), channel_id=1, source_target_pairs={{0,2},{1,3},{2,0},{3,1},{4,6},{5,7},{6,4},{7,5},{8,10},{9,11},{10,... | collective-permute-start | bytes 2359304 | tf_op jit(solution)/shard_map/ppermute | solution.py:27
  184.4 13.3 %collective-permute-start.15 = (bf16[256,1536]{1,0:T(8,128)(2,1)}, bf16[256,1536]{1,0:T(8,128)(2,1)}, u32[]{:S(2)}, u32[]{:S(2)}) collective-permute-start(bf16[256,1536]{1,0:T(8,128)(2,1)} %pad_maximum_fusion.12), channel_id=1, source_target_pairs={{0,4},{1,5},{2,6},{3,7},{4,0},{5,1},{6,2},{7,3},{8,12},{9,13},{10,... | collective-permute-start | bytes 2359304 | tf_op jit(solution)/shard_map/ppermute | solution.py:23
  211.9 13.3 %collective-permute-start.21 = (bf16[128,1536]{1,0:T(8,128)(2,1)S(1)}, bf16[128,1536]{1,0:T(8,128)(2,1)S(1)}, u32[]{:S(2)}, u32[]{:S(2)}) collective-permute-start(bf16[128,1536]{1,0:T(8,128)(2,1)S(1)} %get-tuple-element.35), channel_id=1, source_target_pairs={{0,2},{1,3},{2,0},{3,1},{4,6},{5,7},{6,4},{7,5},{8,10},{9,11},{10,... | collective-permute-start | bytes 1179656 | tf_op jit(solution)/shard_map/ppermute | solution.py:27
  276.0 11.7 %collective-permute-start.32 = (bf16[528,384]{1,0:T(8,128)(2,1)S(1)}, bf16[528,384]{1,0:T(8,128)(2,1)S(1)}, u32[]{:S(2)}, u32[]{:S(2)}) collective-permute-start(bf16[528,384]{1,0:T(8,128)(2,1)S(1)} %get-tuple-element.32), channel_id=1, source_target_pairs={{0,32},{8,40},{16,48},{24,56},{32,0},{40,8},{48,16},{56,24},{64,96... | collective-permute-start | bytes 1216520 | tf_op jit(solution)/shard_map/ppermute | solution.py:315
  277.6 10.1 %collective-permute-start.31 = (bf16[528,384]{1,0:T(8,128)(2,1)S(1)}, bf16[528,384]{1,0:T(8,128)(2,1)S(1)}, u32[]{:S(2)}, u32[]{:S(2)}) collective-permute-start(bf16[528,384]{1,0:T(8,128)(2,1)S(1)} %get-tuple-element.33), channel_id=1, source_target_pairs={{0,48},{8,56},{16,0},{24,8},{32,16},{40,24},{48,32},{56,40},{64,11... | collective-permute-start | bytes 1216520 | tf_op jit(solution)/shard_map/ppermute | solution.py:315
  289.6 28.1 %collective-permute-start.34 = (bf16[4,528,256]{2,1,0:T(8,128)(2,1)}, bf16[4,528,256]{2,1,0:T(8,128)(2,1)}, u32[]{:S(2)}, u32[]{:S(2)}) collective-permute-start(bf16[4,528,256]{2,1,0:T(8,128)(2,1)} %pad_maximum_fusion.4), channel_id=1, source_target_pairs={{0,64},{8,72},{16,80},{24,88},{32,96},{40,104},{48,112},{56,120},{... | collective-permute-start | bytes 3244040 | tf_op jit(solution)/shard_map/ppermute | solution.py:409
  290.9 28.4 %collective-permute-start.36 = (bf16[4,528,256]{2,1,0:T(8,128)(2,1)}, bf16[4,528,256]{2,1,0:T(8,128)(2,1)}, u32[]{:S(2)}, u32[]{:S(2)}) collective-permute-start(bf16[4,528,256]{2,1,0:T(8,128)(2,1)} %pad_maximum_fusion.4), channel_id=1, source_target_pairs={{0,8},{8,0},{16,24},{24,16},{32,40},{40,32},{48,56},{56,48},{64,72... | collective-permute-start | bytes 3244040 | tf_op jit(solution)/shard_map/ppermute | solution.py:321
  317.7 14.8 %collective-permute-start.35 = (bf16[4,528,256]{2,1,0:T(8,128)(2,1)}, bf16[4,528,256]{2,1,0:T(8,128)(2,1)}, u32[]{:S(2)}, u32[]{:S(2)}) collective-permute-start(bf16[4,528,256]{2,1,0:T(8,128)(2,1)} %collective-permute-done.34), channel_id=1, source_target_pairs={{0,8},{8,0},{16,24},{24,16},{32,40},{40,32},{48,56},{56,48},{64,72... | collective-permute-start | bytes 3244040 | tf_op jit(solution)/shard_map/ppermute | solution.py:321
  319.1 56.3 %collective-permute-start.18 = (bf16[256,1536]{1,0:T(8,128)(2,1)}, bf16[256,1536]{1,0:T(8,128)(2,1)}, u32[]{:S(2)}, u32[]{:S(2)}) collective-permute-start(bf16[256,1536]{1,0:T(8,128)(2,1)} %get-tuple-element.39), channel_id=1, source_target_pairs={{0,4},{1,5},{2,6},{3,7},{4,0},{5,1},{6,2},{7,3},{8,12},{9,13},{10,... | collective-permute-start | bytes 2359304 | tf_op jit(solution)/shard_map/ppermute | solution.py:23
  319.1 56.3 %collective-permute-start.16 = (bf16[256,1536]{1,0:T(8,128)(2,1)}, bf16[256,1536]{1,0:T(8,128)(2,1)}, u32[]{:S(2)}, u32[]{:S(2)}) collective-permute-start(bf16[256,1536]{1,0:T(8,128)(2,1)} %get-tuple-element.38), channel_id=1, source_target_pairs={{0,2},{1,3},{2,0},{3,1},{4,6},{5,7},{6,4},{7,5},{8,10},{9,11},{10,... | collective-permute-start | bytes 2359304 | tf_op jit(solution)/shard_map/ppermute | solution.py:27
  367.1 26.4 %collective-permute-start.42 = (bf16[1024,512]{1,0:T(8,128)(2,1)}, bf16[1024,512]{1,0:T(8,128)(2,1)}, u32[]{:S(2)}, u32[]{:S(2)}) collective-permute-start(bf16[1024,512]{1,0:T(8,128)(2,1)} %pad_maximum_fusion.8), channel_id=1, source_target_pairs={{0,4},{1,5},{2,6},{3,7},{4,0},{5,1},{6,2},{7,3},{8,12},{9,13},{10,... | collective-permute-start | bytes 3145736 | tf_op jit(solution)/shard_map/ppermute | solution.py:23
  371.9 27.9 %collective-permute-start.40 = (bf16[1024,512]{1,0:T(8,128)(2,1)S(1)}, bf16[1024,512]{1,0:T(8,128)(2,1)S(1)}, u32[]{:S(2)}, u32[]{:S(2)}) collective-permute-start(bf16[1024,512]{1,0:T(8,128)(2,1)S(1)} %pad_maximum_fusion.7), channel_id=1, source_target_pairs={{0,2},{1,3},{2,0},{3,1},{4,6},{5,7},{6,4},{7,5},{8,10},{9,11},{10,... | collective-permute-start | bytes 3145736 | tf_op jit(solution)/shard_map/ppermute | solution.py:27
  377.0 28.2 %collective-permute-start.20 = (bf16[128,1536]{1,0:T(8,128)(2,1)S(1)}, bf16[128,1536]{1,0:T(8,128)(2,1)S(1)}, u32[]{:S(2)}, u32[]{:S(2)}) collective-permute-start(bf16[128,1536]{1,0:T(8,128)(2,1)S(1)} %get-tuple-element.25), channel_id=1, source_target_pairs={{0,3},{1,0},{2,1},{3,2},{4,7},{5,4},{6,5},{7,6},{8,11},{9,8},{10,9... | collective-permute-start | bytes 1179656 | tf_op jit(solution)/shard_map/ppermute | solution.py:27
  377.1 30.4 %collective-permute-start.19 = (bf16[128,1536]{1,0:T(8,128)(2,1)S(1)}, bf16[128,1536]{1,0:T(8,128)(2,1)S(1)}, u32[]{:S(2)}, u32[]{:S(2)}) collective-permute-start(bf16[128,1536]{1,0:T(8,128)(2,1)S(1)} %get-tuple-element.24), channel_id=1, source_target_pairs={{0,1},{1,2},{2,3},{3,0},{4,5},{5,6},{6,7},{7,4},{8,9},{9,10},{10,1... | collective-permute-start | bytes 1179656 | tf_op jit(solution)/shard_map/ppermute | solution.py:27
  379.1 28.4 %collective-permute-start.17 = (bf16[128,1536]{1,0:T(8,128)(2,1)S(1)}, bf16[128,1536]{1,0:T(8,128)(2,1)S(1)}, u32[]{:S(2)}, u32[]{:S(2)}) collective-permute-start(bf16[128,1536]{1,0:T(8,128)(2,1)S(1)} %get-tuple-element.37), channel_id=1, source_target_pairs={{0,4},{1,5},{2,6},{3,7},{4,0},{5,1},{6,2},{7,3},{8,12},{9,13},{10,... | collective-permute-start | bytes 1179656 | tf_op jit(solution)/shard_map/ppermute | solution.py:23
  394.9 20.0 %collective-permute-start.44 = (bf16[512,512]{1,0:T(8,128)(2,1)S(1)}, bf16[512,512]{1,0:T(8,128)(2,1)S(1)}, u32[]{:S(2)}, u32[]{:S(2)}) collective-permute-start(bf16[512,512]{1,0:T(8,128)(2,1)S(1)} %fusion.19), channel_id=1, source_target_pairs={{0,3},{1,0},{2,1},{3,2},{4,7},{5,4},{6,5},{7,6},{8,11},{9,8},{10,9... | collective-permute-start | bytes 1572872 | tf_op jit(solution)/shard_map/ppermute | solution.py:27
  399.8 18.2 %collective-permute-start.43 = (bf16[512,512]{1,0:T(8,128)(2,1)S(1)}, bf16[512,512]{1,0:T(8,128)(2,1)S(1)}, u32[]{:S(2)}, u32[]{:S(2)}) collective-permute-start(bf16[512,512]{1,0:T(8,128)(2,1)S(1)} %fusion.20), channel_id=1, source_target_pairs={{0,1},{1,2},{2,3},{3,0},{4,5},{5,6},{6,7},{7,4},{8,9},{9,10},{10,1... | collective-permute-start | bytes 1572872 | tf_op jit(solution)/shard_map/ppermute | solution.py:27
  405.1 12.8 %collective-permute-start.41 = (bf16[512,512]{1,0:T(8,128)(2,1)S(1)}, bf16[512,512]{1,0:T(8,128)(2,1)S(1)}, u32[]{:S(2)}, u32[]{:S(2)}) collective-permute-start(bf16[512,512]{1,0:T(8,128)(2,1)S(1)} %fusion.21), channel_id=1, source_target_pairs={{0,4},{1,5},{2,6},{3,7},{4,0},{5,1},{6,2},{7,3},{8,12},{9,13},{10,... | collective-permute-start | bytes 1572872 | tf_op jit(solution)/shard_map/ppermute | solution.py:23
  (45 other events, 542.2 us)
Sparse Core Ops, SparseCore 0:
  40.7 113.5 all-gather.1
